TPU v7x, 32 devices: a whole 2x2x4 slice. The times are simulated.
32 devices in a mesh: seq: 4 (over y, core), chan: 8 (over z, x).
Axes of the slice: x: 2, y: 2, z: 4, core: 2. Of those that a mesh axis runs over, the one named last changes fastest.
Arguments:
- tokens: bfloat16 [512, 4096], P('seq', 'chan'), may hold values from -6 to 6
- in_weight: bfloat16 [4096, 3, 4096], P(None, None, 'chan'), may hold values from -0.09375 to 0.09375
- short_kernel: float32 [3, 3, 4096], P(None, None, 'chan'), may hold values from -3 to 3
- filters: float32 [2, 512, 4096], P(None, 'seq', 'chan'), may hold values from -0.5 to 0.5
- skip_gain: float32 [2, 4096], P(None, 'chan'), may hold values from 0.5 to 1.5
- out_weight: bfloat16 [4096, 4096], P('chan'), may hold values from -0.09375 to 0.09375
- cotangent: bfloat16 [512, 4096], P('seq', 'chan'), may hold values from -6 to 6
Outputs:
- mixed: bfloat16 [512, 4096], P('seq', 'chan')
- token_grad: bfloat16 [512, 4096], P('seq', 'chan')
All inputs are finite; a program needn't handle non-finite values.
Results may differ from a plain program's by a relative error of at most 0.0049.
Values may be sent and summed in bfloat16 or wider, within the bound.
A program may use at most 64 MiB of HBM per device.

v0:
```python
import math

import jax
import jax.numpy as jnp
from jax import lax
from jax.sharding import PartitionSpec as P

PRECISE = lax.Precision.HIGHEST


def swapped(value, axis, apart):
    mask = 2**apart
    pairs = [(source, source ^ mask) for source in range(lax.axis_size(axis))]
    return lax.ppermute(value, axis, pairs)


def passed_along(value, axis, steps):
    count = lax.axis_size(axis)
    first, last = (max(0, -steps), min(count, count - steps))
    return lax.ppermute(value, axis, [(source, source + steps) for source in range(first, last)])


def rotate(real_part, imag_part, turn_angle):
    cosine = jnp.cos(turn_angle)
    sine_part = jnp.sin(turn_angle)
    return (real_part * cosine - imag_part * sine_part, real_part * sine_part + imag_part * cosine)


def block_dft(real_part, imag_part, flip_sign):
    full_shape = real_part.shape
    length = full_shape[-2]
    token_positions = jnp.arange(length, dtype=jnp.int32)
    table_angle = (
        2.0
        * math.pi
        / length
        * (token_positions[:, None] * token_positions[None, :] % length).astype(jnp.float32)
    )
    cosine = jnp.cos(table_angle)
    sine_part = flip_sign * jnp.sin(table_angle)
    summed = cosine + sine_part
    differ = sine_part - cosine
    flat_re = real_part.reshape((-1, length, full_shape[-1]))
    flat_im = imag_part.reshape((-1, length, full_shape[-1]))
    product_one = jnp.einsum("kn,anc->akc", cosine, flat_re + flat_im, precision=PRECISE)
    product_two = jnp.einsum("kn,anc->akc", summed, flat_im, precision=PRECISE)
    product_three = jnp.einsum("kn,anc->akc", differ, flat_re, precision=PRECISE)
    return (
        (product_one - product_two).reshape(full_shape),
        (product_one + product_three).reshape(full_shape),
    )


def twiddle(real_part, imag_part, column, full_length, flip_sign):
    row_ids = jnp.arange(real_part.shape[-2], dtype=jnp.int32)[:, None]
    turn_angle = (
        flip_sign
        * 2.0
        * math.pi
        / full_length
        * (column * row_ids % full_length).astype(jnp.float32)
    )
    return rotate(real_part, imag_part, turn_angle)


def reversed_index(seq_index, levels):
    flipped = jnp.zeros((), jnp.int32)
    for section_bit in range(levels):
        flipped = flipped + seq_index // 2**section_bit % 2 * 2 ** (levels - 1 - section_bit)
    return flipped


def spectrum(signal):
    seq_count = lax.axis_size("seq")
    levels = seq_count.bit_length() - 1
    seq_index = lax.axis_index("seq")
    blocks = signal.shape[1]
    full_length = 2 * seq_count * blocks
    quarter = jnp.arange(2, dtype=jnp.int32)
    lift_angle = -math.pi / seq_count * seq_index.astype(jnp.float32)
    real_part = jnp.stack([signal, signal * jnp.cos(lift_angle)])
    imag_part = jnp.stack([jnp.zeros_like(signal), signal * jnp.sin(lift_angle)])
    for section_bit in reversed(range(levels)):
        half_span = 2**section_bit
        other_re, other_im = swapped((real_part, imag_part), "seq", section_bit)
        is_upper = seq_index // half_span % 2 == 1
        phase_angle = -math.pi / half_span * (seq_index % half_span).astype(jnp.float32)
        diff_re, diff_im = rotate(other_re - real_part, other_im - imag_part, phase_angle)
        real_part = jnp.where(is_upper, diff_re, real_part + other_re)
        imag_part = jnp.where(is_upper, diff_im, imag_part + other_im)
    column = 2 * reversed_index(seq_index, levels) + quarter[:, None, None, None]
    real_part, imag_part = twiddle(real_part, imag_part, column, full_length, -1.0)
    return block_dft(real_part, imag_part, -1.0)


def restore(real_part, imag_part):
    seq_count = lax.axis_size("seq")
    levels = seq_count.bit_length() - 1
    seq_index = lax.axis_index("seq")
    blocks = real_part.shape[-2]
    full_length = 2 * seq_count * blocks
    quarter = jnp.arange(2, dtype=jnp.int32)
    real_part, imag_part = block_dft(real_part, imag_part, 1.0)
    real_part = real_part / blocks
    imag_part = imag_part / blocks
    column = 2 * reversed_index(seq_index, levels) + quarter[:, None, None, None]
    real_part, imag_part = twiddle(real_part, imag_part, column, full_length, 1.0)
    for section_bit in range(levels):
        half_span = 2**section_bit
        other_re, other_im = swapped((real_part, imag_part), "seq", section_bit)
        is_upper = seq_index // half_span % 2 == 1
        phase_angle = math.pi / half_span * (seq_index % half_span).astype(jnp.float32)
        turned_re, turned_im = rotate(other_re, other_im, phase_angle)
        local_rotated_real, own_turn_im = rotate(real_part, imag_part, phase_angle)
        new_re = jnp.where(is_upper, other_re - local_rotated_real, real_part + turned_re)
        new_im = jnp.where(is_upper, other_im - own_turn_im, imag_part + turned_im)
        real_part = 0.5 * new_re
        imag_part = 0.5 * new_im
    lift_angle = math.pi / seq_count * seq_index.astype(jnp.float32)
    return 0.5 * (
        real_part[0] + real_part[1] * jnp.cos(lift_angle) - imag_part[1] * jnp.sin(lift_angle)
    )


def product_of(left_pair, right_pair, conjugate):
    left_re, left_im = left_pair
    right_re, right_im = right_pair
    if conjugate:
        right_im = -right_im
    return (left_re * right_re - left_im * right_im, left_re * right_im + left_im * right_re)


def select_entry(pair, entry):
    return (pair[0][:, entry : entry + 1], pair[1][:, entry : entry + 1])


def on_device(tokens, in_weight, short_kernel, filters, skip_gain, out_weight, cotangent):
    chans = in_weight.shape[2]
    width = in_weight.shape[0]
    blocks = tokens.shape[0]
    flat_in = in_weight.reshape((width, 3 * chans))
    projected = jnp.dot(
        lax.all_gather(tokens, "chan", axis=1, tiled=True),
        flat_in,
        preferred_element_type=jnp.float32,
    )
    projected = projected.reshape((blocks, 3, chans))
    taps = short_kernel.shape[0]
    prior = passed_along(projected[blocks - (taps - 1) :], "seq", 1)
    padded = jnp.concatenate([prior, projected], axis=0)
    shorted = short_kernel[0] * projected
    for tap_index in range(1, taps):
        offset = taps - 1 - tap_index
        shorted = shorted + short_kernel[tap_index] * padded[offset : offset + blocks]
    values = shorted[:, 0]
    gate_one = shorted[:, 1]
    gate_two = shorted[:, 2]
    spectra = spectrum(jnp.stack([filters[0], filters[1], values]))
    conv_one = (
        restore(*product_of(select_entry(spectra, 2), select_entry(spectra, 0), False))[0]
        + skip_gain[0] * values
    )
    first_out = gate_one * conv_one
    first_spec = spectrum(first_out[None])
    conv_two = (
        restore(*product_of(first_spec, select_entry(spectra, 1), False))[0]
        + skip_gain[1] * first_out
    )
    second_order_output = (gate_two * conv_two).astype(jnp.bfloat16)
    picked = out_weight
    mixed = lax.psum_scatter(
        lax.dot_general(
            picked,
            second_order_output,
            (((0,), (1,)), ((), ())),
            preferred_element_type=jnp.float32,
        ),
        "chan",
        scatter_dimension=0,
        tiled=True,
    ).T.astype(jnp.bfloat16)
    grad_two = lax.dot_general(
        lax.all_gather(cotangent, "chan", axis=1, tiled=True),
        out_weight,
        (((1,), (1,)), ((), ())),
        preferred_element_type=jnp.float32,
    )
    grad_gate_two = grad_two * conv_two
    grad_conv_two = grad_two * gate_two
    grad_spec = spectrum(grad_conv_two[None])
    grad_first = (
        restore(*product_of(grad_spec, select_entry(spectra, 1), True))[0]
        + skip_gain[1] * grad_conv_two
    )
    first_gate_gradient = grad_first * conv_one
    grad_conv_one = grad_first * gate_one
    inner_spec = spectrum(grad_conv_one[None])
    grad_values = (
        restore(*product_of(inner_spec, select_entry(spectra, 0), True))[0]
        + skip_gain[0] * grad_conv_one
    )
    grad_short = jnp.stack([grad_values, first_gate_gradient, grad_gate_two], axis=1)
    later = passed_along(grad_short[: taps - 1], "seq", -1)
    padded_grad = jnp.concatenate([grad_short, later], axis=0)
    grad_proj = short_kernel[0] * grad_short
    for tap_index in range(1, taps):
        grad_proj = (
            grad_proj + short_kernel[tap_index] * padded_grad[tap_index : tap_index + blocks]
        )
    grad_proj = grad_proj.astype(jnp.bfloat16)
    grad_flat = grad_proj.reshape((blocks, 3 * chans))
    picked = flat_in
    token_grad = lax.psum_scatter(
        lax.dot_general(
            picked, grad_flat, (((1,), (1,)), ((), ())), preferred_element_type=jnp.float32
        ),
        "chan",
        scatter_dimension=0,
        tiled=True,
    ).T.astype(jnp.bfloat16)
    return (mixed, token_grad)


def solution(mesh):
    in_specs = (
        P("seq", "chan"),
        P(None, None, "chan"),
        P(None, None, "chan"),
        P(None, "seq", "chan"),
        P(None, "chan"),
        P("chan", None),
        P("seq", "chan"),
    )
    out_specs = (P("seq", "chan"), P("seq", "chan"))
    return jax.shard_map(
        on_device, mesh=mesh, in_specs=in_specs, out_specs=out_specs, check_vma=False
    )
```

profile of v0, /device:TPU:0, one launch (start us, length us, event | category | flops | bytes accessed | tf_op | source)
XLA Modules:
  0.0 503.7 jit_solution(16937477585734713768)
XLA Ops:
  8.7 17.0 %copy.86 = bf16[4096,3,512]{0,2,1:T(8,128)(2,1)} copy(bf16[4096,3,512]{2,0,1:T(8,128)(2,1)} %param.8) | data formatting | bytes 25165824 | tf_op args[1]
  25.7 26.6 %all-gather.3.cloned.1.call-done = bf16[128,4096]{1,0:T(8,128)(2,1)} async-done(((bf16[128,512]{1,0:T(8,128)(2,1)}), bf16[128,4096]{1,0:T(8,128)(2,1)}) %all-gather.3.cloned.1.call-update) | async-done | bytes 1048592 | tf_op jit(solution)/shard_map/all_gather | solution.py:143
  52.3 9.2 %fusion.293 = f32[128,1536]{1,0:T(8,128)S(1)} fusion(bf16[128,4096]{1,0:T(8,128)(2,1)} %all-gather.3.cloned.1.call-done, bf16[4096,1536]{0,1:T(8,128)(2,1)} %bitcast.661), kind=kOutput, calls=%fused_computation.434 | convolution fusion | flops 1610612736 | bytes 14417920 | tf_op jit(solution)/shard_map/dot_general | solution.py:142
  61.5 1.8 collective-permute-start
  66.6 3.3 collective-permute-start.1
  71.3 21.6 %all-gather.5.cloned.1.call-done = bf16[128,4096]{1,0:T(8,128)(2,1)} async-done(((bf16[128,512]{1,0:T(8,128)(2,1)}), bf16[128,4096]{1,0:T(8,128)(2,1)}) %all-gather.5.cloned.1.call-update) | async-done | bytes 1048592 | tf_op jit(solution)/shard_map/all_gather | solution.py:183
  92.8 4.0 fusion.294
  101.0 4.5 collective-permute-done.1
  105.5 33.7 %collective-permute-done.2 = f32[2,3,128,512]{3,2,1,0:T(8,128)} collective-permute-done((f32[2,3,128,512]{3,2,1,0:T(8,128)}, f32[2,3,128,512]{3,2,1,0:T(8,128)}, u32[]{:S(2)}, u32[]{:S(2)}) %collective-permute-start.2) | collective-permute-done | bytes 1572896 | tf_op jit(solution)/shard_map/ppermute | solution.py:14
  139.2 4.2 add_select_fusion.2
  143.9 6.5 %collective-permute-done.17 = f32[2,1,128,512]{3,2,1,0:T(8,128)} collective-permute-done((f32[2,1,128,512]{3,2,1,0:T(8,128)}, f32[2,1,128,512]{3,2,1,0:T(8,128)}, u32[]{:S(2)}, u32[]{:S(2)}) %collective-permute-start.17) | collective-permute-done | bytes 524320 | tf_op jit(solution)/shard_map/ppermute | solution.py:14
  150.4 11.2 %collective-permute-done.18 = f32[2,1,128,512]{3,2,0,1:T(8,128)} collective-permute-done((f32[2,1,128,512]{3,2,0,1:T(8,128)}, f32[2,1,128,512]{3,2,0,1:T(8,128)}, u32[]{:S(2)}, u32[]{:S(2)}) %collective-permute-start.18) | collective-permute-done | bytes 524320 | tf_op jit(solution)/shard_map/ppermute | solution.py:14
  168.6 2.0 fusion.5
  170.7 3.0 multiply_add_fusion
  173.9 1.6 copy.91
  175.6 1.6 copy.92
  177.2 3.5 fusion
  180.7 3.0 convolution_add_fusion
  183.8 2.8 convolution_subtract_fusion
  195.2 1.7 collective-permute-start.24
  197.3 12.7 %collective-permute-done.23 = f32[2,1,128,512]{3,2,0,1:T(8,128)} collective-permute-done((f32[2,1,128,512]{3,2,0,1:T(8,128)}, f32[2,1,128,512]{3,2,0,1:T(8,128)}, u32[]{:S(2)}, u32[]{:S(2)}) %collective-permute-start.23) | collective-permute-done | bytes 524320 | tf_op jit(solution)/shard_map/ppermute | solution.py:14
  210.0 10.4 %collective-permute-done.24 = f32[2,1,128,512]{3,2,0,1:T(8,128)} collective-permute-done((f32[2,1,128,512]{3,2,0,1:T(8,128)}, f32[2,1,128,512]{3,2,0,1:T(8,128)}, u32[]{:S(2)}, u32[]{:S(2)}) %collective-permute-start.24) | collective-permute-done | bytes 524320 | tf_op jit(solution)/shard_map/ppermute | solution.py:14
  220.5 1.6 select_multiply_fusion.1
  224.0 1.8 collective-permute-start.26
  225.8 12.7 %collective-permute-done.25 = f32[2,1,128,512]{3,2,0,1:T(8,128)S(1)} collective-permute-done((f32[2,1,128,512]{3,2,0,1:T(8,128)S(1)}, f32[2,1,128,512]{3,2,0,1:T(8,128)S(1)}, u32[]{:S(2)}, u32[]{:S(2)}) %collective-permute-start.25) | collective-permute-done | bytes 524320 | tf_op jit(solution)/shard_map/ppermute | solution.py:14
  238.5 9.5 %collective-permute-done.26 = f32[2,1,128,512]{3,2,0,1:T(8,128)S(1)} collective-permute-done((f32[2,1,128,512]{3,2,0,1:T(8,128)S(1)}, f32[2,1,128,512]{3,2,0,1:T(8,128)S(1)}, u32[]{:S(2)}, u32[]{:S(2)}) %collective-permute-start.26) | collective-permute-done | bytes 524320 | tf_op jit(solution)/shard_map/ppermute | solution.py:14
  251.4 1.5 fusion.30
  260.1 2.1 multiply_subtract_fusion.1
  265.6 1.8 collective-permute-start.8
  267.3 12.7 %collective-permute-done.7 = f32[2,1,128,512]{3,2,0,1:T(8,128)S(1)} collective-permute-done((f32[2,1,128,512]{3,2,0,1:T(8,128)S(1)}, f32[2,1,128,512]{3,2,0,1:T(8,128)S(1)}, u32[]{:S(2)}, u32[]{:S(2)}) %collective-permute-start.7) | collective-permute-done | bytes 524320 | tf_op jit(solution)/shard_map/ppermute | solution.py:14
  280.1 10.4 %collective-permute-done.8 = f32[2,1,128,512]{3,2,0,1:T(8,128)S(1)} collective-permute-done((f32[2,1,128,512]{3,2,0,1:T(8,128)S(1)}, f32[2,1,128,512]{3,2,0,1:T(8,128)S(1)}, u32[]{:S(2)}, u32[]{:S(2)}) %collective-permute-start.8) | collective-permute-done | bytes 524320 | tf_op jit(solution)/shard_map/ppermute | solution.py:14
  291.6 1.8 collective-permute-start.10
  293.4 12.7 %collective-permute-done.9 = f32[2,1,128,512]{3,2,0,1:T(8,128)S(1)} collective-permute-done((f32[2,1,128,512]{3,2,0,1:T(8,128)S(1)}, f32[2,1,128,512]{3,2,0,1:T(8,128)S(1)}, u32[]{:S(2)}, u32[]{:S(2)}) %collective-permute-start.9) | collective-permute-done | bytes 524320 | tf_op jit(solution)/shard_map/ppermute | solution.py:14
  306.1 9.5 %collective-permute-done.10 = f32[2,1,128,512]{3,2,0,1:T(8,128)S(1)} collective-permute-done((f32[2,1,128,512]{3,2,0,1:T(8,128)S(1)}, f32[2,1,128,512]{3,2,0,1:T(8,128)S(1)}, u32[]{:S(2)}, u32[]{:S(2)}) %collective-permute-start.10) | collective-permute-done | bytes 524320 | tf_op jit(solution)/shard_map/ppermute | solution.py:14
  329.4 1.7 collective-permute-start.16
  331.1 12.7 %collective-permute-done.15 = f32[2,1,128,512]{3,2,0,1:T(8,128)S(1)} collective-permute-done((f32[2,1,128,512]{3,2,0,1:T(8,128)S(1)}, f32[2,1,128,512]{3,2,0,1:T(8,128)S(1)}, u32[]{:S(2)}, u32[]{:S(2)}) %collective-permute-start.15) | collective-permute-done | bytes 524320 | tf_op jit(solution)/shard_map/ppermute | solution.py:14
  343.8 10.4 %collective-permute-done.16 = f32[2,1,128,512]{3,2,0,1:T(8,128)S(1)} collective-permute-done((f32[2,1,128,512]{3,2,0,1:T(8,128)S(1)}, f32[2,1,128,512]{3,2,0,1:T(8,128)S(1)}, u32[]{:S(2)}, u32[]{:S(2)}) %collective-permute-start.16) | collective-permute-done | bytes 524320 | tf_op jit(solution)/shard_map/ppermute | solution.py:14
  354.9 1.6 copy-done
  356.5 2.0 convolution_bitcast_fusion.1
  362.8 1.7 collective-permute-start.32
  364.6 12.7 %collective-permute-done.31 = f32[2,1,128,512]{3,2,0,1:T(8,128)S(1)} collective-permute-done((f32[2,1,128,512]{3,2,0,1:T(8,128)S(1)}, f32[2,1,128,512]{3,2,0,1:T(8,128)S(1)}, u32[]{:S(2)}, u32[]{:S(2)}) %collective-permute-start.31) | collective-permute-done | bytes 524320 | tf_op jit(solution)/shard_map/ppermute | solution.py:14
  377.3 10.4 %collective-permute-done.32 = f32[2,1,128,512]{3,2,0,1:T(8,128)S(1)} collective-permute-done((f32[2,1,128,512]{3,2,0,1:T(8,128)S(1)}, f32[2,1,128,512]{3,2,0,1:T(8,128)S(1)}, u32[]{:S(2)}, u32[]{:S(2)}) %collective-permute-start.32) | collective-permute-done | bytes 524320 | tf_op jit(solution)/shard_map/ppermute | solution.py:14
  389.6 1.8 collective-permute-done.33
  391.5 10.1 %convolution_bitcast_fusion = f32[4096,128]{0,1:T(8,128)} fusion(bf16[4096,3,512]{2,0,1:T(8,128)(2,1)} %param.8, f32[130,3,512]{2,0,1:T(8,128)S(1)} %pad_maximum_fusion.1, f32[3,512]{1,0:T(4,128)S(1)} %get-tuple-element.67, f32[3,512]{1,0:T(4,128)S(1)} %get-tuple-element.68, f32[3,512]{1,0:T(4,128)S(1)} %get-tuple-element.66, ...), kind=kOutput, calls=%fused_computation | convolution fusion | flops 1612185600 | bytes 17063936 | tf_op jit(solution)/shard_map/dot_general | solution.py:214
  401.6 23.0 %reduce-scatter.3.cloned.1.call-done = f32[512,128]{0,1:T(8,128)} async-done(((f32[4096,128]{0,1:T(8,128)}), f32[512,128]{0,1:T(8,128)}) %reduce-scatter.3.cloned.1.call-update) | async-done | bytes 262160 | tf_op jit(solution)/shard_map/reduce_scatter | solution.py:171
  424.6 1.6 convert_bitcast_fusion.1
  426.2 68.9 %reduce-scatter.5.cloned.1.call-done = f32[512,128]{0,1:T(8,128)} async-done(((f32[4096,128]{0,1:T(8,128)}), f32[512,128]{0,1:T(8,128)}) %reduce-scatter.5.cloned.1.call-update) | async-done | bytes 262160 | tf_op jit(solution)/shard_map/reduce_scatter | solution.py:213
  495.1 1.6 convert_bitcast_fusion
  (161 shorter events, 63.3 us)
Async XLA Ops:
  7.2 45.1 %all-gather.3.cloned.1.call-start = ((), (), s32[]{:S(2)}) async-start(), calls=%async_computation.2 | async-start | bytes 1179648 | tf_op jit(solution)/shard_map/all_gather | solution.py:143
  7.9 84.9 %all-gather.5.cloned.1.call-start = ((), (), s32[]{:S(2)}) async-start(), calls=%async_computation.4 | async-start | bytes 1179648 | tf_op jit(solution)/shard_map/all_gather | solution.py:183
  8.6 416.0 %reduce-scatter.3.cloned.1.call-start = ((), (), s32[]{:S(2)}) async-start(), calls=%async_computation.3 | async-start | bytes 2359296 | tf_op jit(solution)/shard_map/reduce_scatter | solution.py:171
  52.3 11.0 %copy-start.20 = (f32[3,3,512]{2,1,0:T(4,128)S(1)}, f32[3,3,512]{2,1,0:T(4,128)}, u32[]{:S(2)}) copy-start(f32[3,3,512]{2,1,0:T(4,128)} %param.9) | copy-start | bytes 55300
  61.5 2.5 collective-permute-start
  64.3 32.6 %copy-start.1 = (f32[128,3,512]{2,0,1:T(8,128)}, f32[128,3,512]{2,0,1:T(8,128)S(1)}, u32[]{:S(2)}) copy-start(f32[128,3,512]{2,0,1:T(8,128)S(1)} %fusion.11) | copy-start | bytes 2359300
  66.6 38.9 %collective-permute-start.1 = (f32[2,3,128,512]{3,2,1,0:T(8,128)}, f32[2,3,128,512]{3,2,1,0:T(8,128)}, u32[]{:S(2)}, u32[]{:S(2)}) collective-permute-start(f32[2,3,128,512]{3,2,1,0:T(8,128)} %pad_maximum_fusion), channel_id=1, source_target_pairs={{0,16},{8,24},{16,0},{24,8},{1,17},{9,25},{17,1},{25,9},{2,18},{10... | collective-permute-start | bytes 4718600 | tf_op jit(solution)/shard_map/ppermute | solution.py:14
  71.2 67.9 %collective-permute-start.2 = (f32[2,3,128,512]{3,2,1,0:T(8,128)}, f32[2,3,128,512]{3,2,1,0:T(8,128)}, u32[]{:S(2)}, u32[]{:S(2)}) collective-permute-start(f32[2,3,128,512]{3,2,1,0:T(8,128)} %stack.71), channel_id=1, source_target_pairs={{0,16},{8,24},{16,0},{24,8},{1,17},{9,25},{17,1},{25,9},{2,18},{10... | collective-permute-start | bytes 4718600 | tf_op jit(solution)/shard_map/ppermute | solution.py:14
  96.9 3.4 copy-start.14
  97.9 52.5 %collective-permute-start.17 = (f32[2,1,128,512]{3,2,1,0:T(8,128)}, f32[2,1,128,512]{3,2,1,0:T(8,128)}, u32[]{:S(2)}, u32[]{:S(2)}) collective-permute-start(f32[2,1,128,512]{3,2,1,0:T(8,128)} %pad_maximum_fusion.6), channel_id=1, source_target_pairs={{0,16},{8,24},{16,0},{24,8},{1,17},{9,25},{17,1},{25,9},{2,18},{10... | collective-permute-start | bytes 1572872 | tf_op jit(solution)/shard_map/ppermute | solution.py:14
  100.3 61.3 %collective-permute-start.18 = (f32[2,1,128,512]{3,2,0,1:T(8,128)}, f32[2,1,128,512]{3,2,0,1:T(8,128)}, u32[]{:S(2)}, u32[]{:S(2)}) collective-permute-start(f32[2,1,128,512]{3,2,0,1:T(8,128)} %pad_bitcast_fusion.2), channel_id=1, source_target_pairs={{0,16},{8,24},{16,0},{24,8},{1,17},{9,25},{17,1},{25,9},{2,18},{10... | collective-permute-start | bytes 1572872 | tf_op jit(solution)/shard_map/ppermute | solution.py:14
  101.0 60.7 %copy-start.13 = (f32[1,1,128,512]{3,2,1,0:T(8,128)S(1)}, f32[1,1,128,512]{3,2,1,0:T(8,128)}, u32[]{:S(2)}) copy-start(f32[1,1,128,512]{3,2,1,0:T(8,128)} %copy-done.12) | copy-start | bytes 786436
  143.4 27.3 %collective-permute-start.3 = (f32[2,3,128,512]{3,2,1,0:T(8,128)}, f32[2,3,128,512]{3,2,1,0:T(8,128)S(1)}, u32[]{:S(2)}, u32[]{:S(2)}) collective-permute-start(f32[2,3,128,512]{3,2,1,0:T(8,128)} %get-tuple-element.33), channel_id=1, source_target_pairs={{0,8},{8,0},{16,24},{24,16},{1,9},{9,1},{17,25},{25,17},{2,10},{10... | collective-permute-start | bytes 4718600 | tf_op jit(solution)/shard_map/ppermute | solution.py:14
  143.5 27.2 %collective-permute-start.4 = (f32[2,3,128,512]{3,2,1,0:T(8,128)}, f32[2,3,128,512]{3,2,1,0:T(8,128)}, u32[]{:S(2)}, u32[]{:S(2)}) collective-permute-start(f32[2,3,128,512]{3,2,1,0:T(8,128)} %get-tuple-element.32), channel_id=1, source_target_pairs={{0,8},{8,0},{16,24},{24,16},{1,9},{9,1},{17,25},{25,17},{2,10},{10... | collective-permute-start | bytes 4718600 | tf_op jit(solution)/shard_map/ppermute | solution.py:14
  163.1 2.0 collective-permute-start.19
  163.2 2.7 collective-permute-start.20
  167.2 3.4 copy-start.3
  167.2 3.4 copy-start.5
  190.7 2.0 collective-permute-start.21
  190.9 6.4 %copy-start.21 = (f32[2,512]{1,0:T(2,128)S(1)}, f32[2,512]{1,0:T(2,128)}, u32[]{:S(2)}) copy-start(f32[2,512]{1,0:T(2,128)} %param.11) | copy-start | bytes 12292
  190.9 2.5 collective-permute-start.22
  194.9 27.1 %copy-start.2 = (f32[128,3,512]{2,0,1:T(8,128)S(1)}, f32[128,3,512]{2,0,1:T(8,128)}, u32[]{:S(2)}) copy-start(f32[128,3,512]{2,0,1:T(8,128)} %copy-done.1) | copy-start | bytes 2359300
  194.9 15.1 %collective-permute-start.23 = (f32[2,1,128,512]{3,2,0,1:T(8,128)}, f32[2,1,128,512]{3,2,0,1:T(8,128)}, u32[]{:S(2)}, u32[]{:S(2)}) collective-permute-start(f32[2,1,128,512]{3,2,0,1:T(8,128)} %get-tuple-element.48), channel_id=1, source_target_pairs={{0,16},{8,24},{16,0},{24,8},{1,17},{9,25},{17,1},{25,9},{2,18},{10... | collective-permute-start | bytes 1572872 | tf_op jit(solution)/shard_map/ppermute | solution.py:14
  195.2 25.2 %collective-permute-start.24 = (f32[2,1,128,512]{3,2,0,1:T(8,128)}, f32[2,1,128,512]{3,2,0,1:T(8,128)}, u32[]{:S(2)}, u32[]{:S(2)}) collective-permute-start(f32[2,1,128,512]{3,2,0,1:T(8,128)} %get-tuple-element.13), channel_id=1, source_target_pairs={{0,16},{8,24},{16,0},{24,8},{1,17},{9,25},{17,1},{25,9},{2,18},{10... | collective-permute-start | bytes 1572872 | tf_op jit(solution)/shard_map/ppermute | solution.py:14
  197.3 24.8 %copy-start.11 = (f32[2,1,128,512]{3,2,0,1:T(8,128)S(1)}, f32[2,1,128,512]{3,2,0,1:T(8,128)}, u32[]{:S(2)}) copy-start(f32[2,1,128,512]{3,2,0,1:T(8,128)} %get-tuple-element.49) | copy-start | bytes 1572868
  223.6 14.9 %collective-permute-start.25 = (f32[2,1,128,512]{3,2,0,1:T(8,128)S(1)}, f32[2,1,128,512]{3,2,0,1:T(8,128)S(1)}, u32[]{:S(2)}, u32[]{:S(2)}) collective-permute-start(f32[2,1,128,512]{3,2,0,1:T(8,128)S(1)} %maximum_bitcast_fusion.1), channel_id=1, source_target_pairs={{0,16},{8,24},{16,0},{24,8},{1,17},{9,25},{17,1},{25,9},{2,18},{10... | collective-permute-start | bytes 1572872 | tf_op jit(solution)/shard_map/ppermute | solution.py:14
  224.0 24.0 %collective-permute-start.26 = (f32[2,1,128,512]{3,2,0,1:T(8,128)S(1)}, f32[2,1,128,512]{3,2,0,1:T(8,128)S(1)}, u32[]{:S(2)}, u32[]{:S(2)}) collective-permute-start(f32[2,1,128,512]{3,2,0,1:T(8,128)S(1)} %pad_bitcast_fusion), channel_id=1, source_target_pairs={{0,16},{8,24},{16,0},{24,8},{1,17},{9,25},{17,1},{25,9},{2,18},{10... | collective-permute-start | bytes 1572872 | tf_op jit(solution)/shard_map/ppermute | solution.py:14
  248.2 2.0 collective-permute-start.27
  248.5 2.4 collective-permute-start.28
  262.2 1.9 collective-permute-start.5
  262.3 2.5 collective-permute-start.6
  265.2 14.8 %collective-permute-start.7 = (f32[2,1,128,512]{3,2,0,1:T(8,128)S(1)}, f32[2,1,128,512]{3,2,0,1:T(8,128)S(1)}, u32[]{:S(2)}, u32[]{:S(2)}) collective-permute-start(f32[2,1,128,512]{3,2,0,1:T(8,128)S(1)} %get-tuple-element.46), channel_id=1, source_target_pairs={{0,16},{8,24},{16,0},{24,8},{1,17},{9,25},{17,1},{25,9},{2,18},{10... | collective-permute-start | bytes 1572872 | tf_op jit(solution)/shard_map/ppermute | solution.py:14
  265.6 24.9 %collective-permute-start.8 = (f32[2,1,128,512]{3,2,0,1:T(8,128)S(1)}, f32[2,1,128,512]{3,2,0,1:T(8,128)S(1)}, u32[]{:S(2)}, u32[]{:S(2)}) collective-permute-start(f32[2,1,128,512]{3,2,0,1:T(8,128)S(1)} %get-tuple-element.27), channel_id=1, source_target_pairs={{0,16},{8,24},{16,0},{24,8},{1,17},{9,25},{17,1},{25,9},{2,18},{10... | collective-permute-start | bytes 1572872 | tf_op jit(solution)/shard_map/ppermute | solution.py:14
  291.2 14.9 %collective-permute-start.9 = (f32[2,1,128,512]{3,2,0,1:T(8,128)S(1)}, f32[2,1,128,512]{3,2,0,1:T(8,128)S(1)}, u32[]{:S(2)}, u32[]{:S(2)}) collective-permute-start(f32[2,1,128,512]{3,2,0,1:T(8,128)S(1)} %pad_maximum_fusion.5), channel_id=1, source_target_pairs={{0,16},{8,24},{16,0},{24,8},{1,17},{9,25},{17,1},{25,9},{2,18},{10... | collective-permute-start | bytes 1572872 | tf_op jit(solution)/shard_map/ppermute | solution.py:14
  291.6 24.0 %collective-permute-start.10 = (f32[2,1,128,512]{3,2,0,1:T(8,128)S(1)}, f32[2,1,128,512]{3,2,0,1:T(8,128)S(1)}, u32[]{:S(2)}, u32[]{:S(2)}) collective-permute-start(f32[2,1,128,512]{3,2,0,1:T(8,128)S(1)} %pad_bitcast_fusion.1), channel_id=1, source_target_pairs={{0,16},{8,24},{16,0},{24,8},{1,17},{9,25},{17,1},{25,9},{2,18},{10... | collective-permute-start | bytes 1572872 | tf_op jit(solution)/shard_map/ppermute | solution.py:14
  315.9 2.0 collective-permute-start.11
  316.2 2.4 collective-permute-start.12
  326.0 2.0 collective-permute-start.13
  326.2 2.5 collective-permute-start.14
  329.0 25.5 %copy-start.15 = (f32[128,512]{1,0:T(8,128)S(1)}, f32[128,512]{1,0:T(8,128)}, u32[]{:S(2)}) copy-start(f32[128,512]{1,0:T(8,128)} %copy-done.14) | copy-start | bytes 786436
  329.0 14.8 %collective-permute-start.15 = (f32[2,1,128,512]{3,2,0,1:T(8,128)S(1)}, f32[2,1,128,512]{3,2,0,1:T(8,128)S(1)}, u32[]{:S(2)}, u32[]{:S(2)}) collective-permute-start(f32[2,1,128,512]{3,2,0,1:T(8,128)S(1)} %get-tuple-element.44), channel_id=1, source_target_pairs={{0,16},{8,24},{16,0},{24,8},{1,17},{9,25},{17,1},{25,9},{2,18},{10... | collective-permute-start | bytes 1572872 | tf_op jit(solution)/shard_map/ppermute | solution.py:14
  329.4 24.9 %collective-permute-start.16 = (f32[2,1,128,512]{3,2,0,1:T(8,128)S(1)}, f32[2,1,128,512]{3,2,0,1:T(8,128)S(1)}, u32[]{:S(2)}, u32[]{:S(2)}) collective-permute-start(f32[2,1,128,512]{3,2,0,1:T(8,128)S(1)} %get-tuple-element.21), channel_id=1, source_target_pairs={{0,16},{8,24},{16,0},{24,8},{1,17},{9,25},{17,1},{25,9},{2,18},{10... | collective-permute-start | bytes 1572872 | tf_op jit(solution)/shard_map/ppermute | solution.py:14
  358.5 136.6 %reduce-scatter.5.cloned.1.call-start = ((), (), s32[]{:S(2)}) async-start(), calls=%async_computation.5 | async-start | bytes 2359296 | tf_op jit(solution)/shard_map/reduce_scatter | solution.py:213
  359.5 1.9 collective-permute-start.29
  359.7 2.5 collective-permute-start.30
  362.5 14.8 %collective-permute-start.31 = (f32[2,1,128,512]{3,2,0,1:T(8,128)S(1)}, f32[2,1,128,512]{3,2,0,1:T(8,128)S(1)}, u32[]{:S(2)}, u32[]{:S(2)}) collective-permute-start(f32[2,1,128,512]{3,2,0,1:T(8,128)S(1)} %get-tuple-element.2), channel_id=1, source_target_pairs={{0,16},{8,24},{16,0},{24,8},{1,17},{9,25},{17,1},{25,9},{2,18},{10... | collective-permute-start | bytes 1572872 | tf_op jit(solution)/shard_map/ppermute | solution.py:14
  362.8 24.9 %collective-permute-start.32 = (f32[2,1,128,512]{3,2,0,1:T(8,128)S(1)}, f32[2,1,128,512]{3,2,0,1:T(8,128)S(1)}, u32[]{:S(2)}, u32[]{:S(2)}) collective-permute-start(f32[2,1,128,512]{3,2,0,1:T(8,128)S(1)} %get-tuple-element.42), channel_id=1, source_target_pairs={{0,16},{8,24},{16,0},{24,8},{1,17},{9,25},{17,1},{25,9},{2,18},{10... | collective-permute-start | bytes 1572872 | tf_op jit(solution)/shard_map/ppermute | solution.py:14
  388.3 3.1 collective-permute-start.33
  (12 other events, 25.4 us)
Sparse Core Ops, SparseCore 0:
  10.0 42.2 all-gather.2
  54.4 38.4 all-gather.4
  358.6 65.9 reduce-scatter.2
  428.0 67.0 reduce-scatter.4
where the time goes:
time: 508 us; the launch traced here: 504 us
  waiting for transfers between devices  351 us (69%)
  matrix products  59.7 us (12%)
  local copies, waits for them, and re-layouts  26.5 us (5%)
  starting transfers between devices  25.5 us (5%)
  other arithmetic  25.5 us (5%)
  between operations  15.6 us (3%)
    ppermute x32, waiting for transfers between devices, swapped(): return lax.ppermute(value, axis, pairs)  208 us
    reduce_scatter x1, waiting for transfers between devices, on_device(): lax.psum_scatter(lax.dot_general(picked, grad_flat, (((1,), (1,)), ((), (...  68.9 us
    all_gather x1, waiting for transfers between devices, on_device(): lax.all_gather(tokens, 'chan', axis=1, tiled=True)  26.6 us
    reduce_scatter x1, waiting for transfers between devices, on_device(): lax.psum_scatter(lax.dot_general(picked, second_order_output, (((0,), (1,...  23 us
    ppermute x32, starting transfers between devices, swapped(): return lax.ppermute(value, axis, pairs)  22.3 us
    all_gather x1, waiting for transfers between devices, on_device(): lax.all_gather(cotangent, 'chan', axis=1, tiled=True)  21.6 us
    unnamed x45, local copies, waits for them, and re-layouts  20.4 us
    dot_general x8, matrix products, block_dft(): jnp.einsum('kn,anc->akc', differ, flat_re, precision=PRECISE)  11.8 us
  transfers between devices with their start and end apart: 38, of which 35 were waited for; matrix products, arithmetic and copies ran while one was open for 12% of the time, Pallas kernels for 0%

commit v1 on v0

v1 whole, which is shorter than its diff:
```python
import math

import jax
import jax.numpy as jnp
import numpy as np
from jax import lax
from jax.sharding import PartitionSpec as P

FINE = lax.Precision.HIGH


def odd_table(length):
    steps = np.arange(length, dtype=np.int64)
    turn = (2 * steps[:, None] + 1) * steps[None, :] % (4 * length)
    angle = turn.astype(np.float64) * (math.pi / (2 * length))
    return np.concatenate([np.cos(angle), -np.sin(angle)]).astype(np.float32)


def forward(table, signal):
    return jnp.dot(table, signal, precision=FINE)


def inverse(table, spec):
    length = table.shape[1]
    full = lax.dot_general(table, spec, (((0,), (0,)), ((), ())), precision=FINE)
    return full * (1.0 / length)


def times(left, right, conjugate):
    half = left.shape[0] // 2
    a, b = left[:half], left[half:]
    c, d = right[:half], right[half:]
    if conjugate:
        d = -d
    return jnp.concatenate([a * c - b * d, a * d + b * c])


def lag(array, by):
    return jnp.pad(array, ((by, 0), (0, 0)))[: array.shape[0]]


def lead(array, by):
    return jnp.pad(array, ((0, by), (0, 0)))[by:]


def middle(projected, grad_two, taps, filters, skip, table):
    count = taps.shape[0]
    shorted = []
    for j in range(3):
        total = taps[0, j] * projected[j]
        for a in range(1, count):
            total = total + taps[a, j] * lag(projected[j], a)
        shorted.append(total)
    values, gate_one, gate_two = shorted
    spec_one = forward(table, filters[0])
    spec_two = forward(table, filters[1])
    conv_one = inverse(table, times(forward(table, values), spec_one, False)) + skip[0] * values
    first_out = gate_one * conv_one
    conv_two = (
        inverse(table, times(forward(table, first_out), spec_two, False)) + skip[1] * first_out
    )
    second_out = (gate_two * conv_two).astype(jnp.bfloat16)
    grad_gate_two = grad_two * conv_two
    grad_conv_two = grad_two * gate_two
    grad_first = (
        inverse(table, times(forward(table, grad_conv_two), spec_two, True))
        + skip[1] * grad_conv_two
    )
    grad_gate_one = grad_first * conv_one
    grad_conv_one = grad_first * gate_one
    grad_values = (
        inverse(table, times(forward(table, grad_conv_one), spec_one, True))
        + skip[0] * grad_conv_one
    )
    grads = []
    for j, g in enumerate((grad_values, grad_gate_one, grad_gate_two)):
        total = taps[0, j] * g
        for a in range(1, count):
            total = total + taps[a, j] * lead(g, a)
        grads.append(total.astype(jnp.bfloat16))
    return second_out, jnp.stack(grads)


def swap_in(array):
    return lax.all_to_all(array, "seq", array.ndim - 1, array.ndim - 2, tiled=True)


def swap_out(array):
    return lax.all_to_all(array, "seq", array.ndim - 2, array.ndim - 1, tiled=True)


def share(partial):
    count = lax.axis_size("chan")
    rows, width = partial.shape
    sent = partial.astype(jnp.bfloat16).reshape(rows, count, width // count).transpose(1, 0, 2)
    got = lax.all_to_all(sent, "chan", 0, 0, tiled=True)
    return jnp.sum(got.astype(jnp.float32), axis=0).astype(jnp.bfloat16)


def on_device(tokens, in_weight, short_kernel, filters, skip_gain, out_weight, cotangent):
    seq_count = lax.axis_size("seq")
    chans = in_weight.shape[2]
    part = chans // seq_count
    start = lax.axis_index("seq") * part
    weights = jnp.transpose(in_weight, (1, 0, 2))
    table = jnp.asarray(odd_table(tokens.shape[0] * seq_count))
    taps = lax.dynamic_slice_in_dim(short_kernel, start, part, 2)
    skip = lax.dynamic_slice_in_dim(skip_gain, start, part, 1)
    rows = lax.all_gather(tokens, "chan", axis=1, tiled=True)
    grad_rows = lax.all_gather(cotangent, "chan", axis=1, tiled=True)
    local_filters = swap_in(filters)
    projected = jnp.stack(
        [jnp.dot(rows, weights[j], preferred_element_type=jnp.float32) for j in range(3)]
    )
    grad_two = lax.dot_general(
        grad_rows, out_weight, (((1,), (1,)), ((), ())), preferred_element_type=jnp.float32
    )
    projected = swap_in(projected)
    grad_two = swap_in(grad_two)
    second_out, grads = middle(projected, grad_two, taps, local_filters, skip, table)
    second_out = swap_out(second_out)
    grads = swap_out(grads)
    mixed = share(jnp.dot(second_out, out_weight, preferred_element_type=jnp.float32))
    total = 0.0
    for j in range(3):
        total = total + lax.dot_general(
            grads[j], weights[j], (((1,), (1,)), ((), ())), preferred_element_type=jnp.float32
        )
    return mixed, share(total)


def solution(mesh):
    in_specs = (
        P("seq", "chan"),
        P(None, None, "chan"),
        P(None, None, "chan"),
        P(None, "seq", "chan"),
        P(None, "chan"),
        P("chan", None),
        P("seq", "chan"),
    )
    out_specs = (P("seq", "chan"), P("seq", "chan"))
    return jax.shard_map(
        on_device, mesh=mesh, in_specs=in_specs, out_specs=out_specs, check_vma=False
    )
```

time: 508 us -> 209 us (0.41)
  waiting for transfers between devices: 351 us -> 103 us
  other arithmetic: 25.5 us -> 4.22 us
  matrix products: 59.7 us -> 46.3 us
  local copies, waits for them, and re-layouts: 26.5 us -> 13.3 us
    ppermute x34 -> x0, waiting for transfers between devices: 209 us -> none  [the longest x32 208 us: swapped(): return lax.ppermute(value, axis, pairs)]
    reduce_scatter x2 -> x0, waiting for transfers between devices: 91.9 us -> none  [the longest x1 68.9 us: on_device(): lax.psum_scatter(lax.dot_general(picked, grad_flat, (((1,), (1,)), ((), (...]
    all_to_all x0 -> x7, waiting for transfers between devices: none -> 49.9 us  [the longest x2 38 us: share(): got = lax.all_to_all(sent, 'chan', 0, 0, tiled=True)]
    all_to_all x0 -> x7, starting transfers between devices: none -> 25.9 us  [the longest x3 11.8 us: swap_in(): lax.all_to_all(array, 'seq', array.ndim - 1, array.ndim - 2, tiled=True)]
    ppermute x34 -> x0, starting transfers between devices: 25.4 us -> none  [the longest x32 22.3 us: swapped(): return lax.ppermute(value, axis, pairs)]
    dot_general x28 -> x21, matrix products: 59.7 us -> 41.8 us  [the longest x3 11.2 us: on_device(): lax.dot_general(grads[j], weights[j], (((1,), (1,)), ((), ())), preferred...]
    unnamed x45 -> x60, local copies, waits for them, and re-layouts: 20.4 us -> 4.42 us
    select_n x11 -> x0, other arithmetic: 8.67 us -> none  [the longest x5 5.07 us: spectrum(): imag_part = jnp.where(is_upper, diff_im, imag_part + other_im)]
  transfers between devices with their start and end apart: 38 -> 9, of which waited for: 35 -> 6; matrix products, arithmetic and copies ran while one was open for 12% -> 28% of each run, Pallas kernels for 0% -> 0%
where the time goes in v1:
time: 209 us; the launch traced here: 208 us
  waiting for transfers between devices  103 us (49%)
  matrix products  46.3 us (22%)
  starting transfers between devices  26 us (12%)
  between operations  14.7 us (7%)
  local copies, waits for them, and re-layouts  13.3 us (6%)
  other arithmetic  4.22 us (2%)
    all_to_all x2, waiting for transfers between devices, share(): got = lax.all_to_all(sent, 'chan', 0, 0, tiled=True)  38 us
    all_gather x1, waiting for transfers between devices, on_device(): rows = lax.all_gather(tokens, 'chan', axis=1, tiled=True)  27.1 us
    all_gather x1, waiting for transfers between devices, on_device(): grad_rows = lax.all_gather(cotangent, 'chan', axis=1, tiled=True)  24.5 us
    all_to_all x3, starting transfers between devices, swap_in(): lax.all_to_all(array, 'seq', array.ndim - 1, array.ndim - 2, tiled=True)  11.8 us
    dot_general x3, matrix products, on_device(): lax.dot_general(grads[j], weights[j], (((1,), (1,)), ((), ())), preferred...  11.2 us
    dot_general x8, matrix products, inverse(): lax.dot_general(table, spec, (((0,), (0,)), ((), ())), precision=FINE)  9.78 us
    dot_general x3, matrix products, on_device(): jnp.dot(rows, weights[j], preferred_element_type=jnp.float32)  9.26 us
    dot_general x6, matrix products, forward(): return jnp.dot(table, signal, precision=FINE)  8.64 us
  transfers between devices with their start and end apart: 9, of which 6 were waited for; matrix products, arithmetic and copies ran while one was open for 28% of the time, Pallas kernels for 0%

profile of v1, /device:TPU:0, one launch (start us, length us, event | category | flops | bytes accessed | tf_op | source)
XLA Modules:
  0.0 207.5 jit_solution(8016526007566932830)
XLA Ops:
  7.2 0.7 all-gather.3.cloned.1.call-update
  7.9 2.0 copy.43
  10.0 4.2 %all-to-all-start.1 = ((f32[2,128,512]{1,0,2:T(2,128)}), f32[2,128,512]{1,0,2:T(2,128)S(1)}, u32[]{:S(2)}, u32[]{:S(2)}) async-start(f32[2,128,512]{1,0,2:T(2,128)} %copy.43), calls=%async_computation.1 | async-start | bytes 1048576 | tf_op jit(solution)/shard_map/all_to_all | solution.py:85
  14.2 0.7 all-gather.5.cloned.1.call-update
  15.0 0.9 fusion.121
  16.0 7.1 %all-to-all-done.1 = f32[2,128,512]{1,0,2:T(2,128)S(1)} async-done(((f32[2,128,512]{1,0,2:T(2,128)}), f32[2,128,512]{1,0,2:T(2,128)S(1)}, u32[]{:S(2)}, u32[]{:S(2)}) %all-to-all-start.1) | async-done | bytes 524320 | tf_op jit(solution)/shard_map/all_to_all | solution.py:85
  23.4 1.8 fusion.134
  25.2 27.1 %all-gather.3.cloned.1.call-done = bf16[128,4096]{1,0:T(8,128)(2,1)} async-done(((bf16[128,512]{1,0:T(8,128)(2,1)}), bf16[128,4096]{1,0:T(8,128)(2,1)}) %all-gather.3.cloned.1.call-update) | async-done | bytes 1048592 | tf_op jit(solution)/shard_map/all_gather | solution.py:109
  52.3 3.3 %fusion.5 = f32[1,128,512]{2,1,0:T(8,128)S(1)} fusion(bf16[128,4096]{1,0:T(8,128)(2,1)} %all-gather.3.cloned.1.call-done, bf16[3,4096,512]{2,1,0:T(8,128)(2,1)} %bitcast.172), kind=kOutput, calls=%fused_computation.11 | convolution fusion | flops 536870912 | bytes 5505024 | tf_op jit(solution)/shard_map/dot_general | solution.py:113
  55.7 3.0 %fusion.6 = f32[1,128,512]{2,1,0:T(8,128)S(1)} fusion(bf16[128,4096]{1,0:T(8,128)(2,1)S(1)} %copy-done.27, bf16[3,4096,512]{2,1,0:T(8,128)(2,1)} %bitcast.173), kind=kOutput, calls=%fused_computation.12 | convolution fusion | flops 536870912 | bytes 5505024 | tf_op jit(solution)/shard_map/dot_general | solution.py:113
  58.6 3.0 %fusion.7 = f32[1,128,512]{2,1,0:T(8,128)S(1)} fusion(bf16[128,4096]{1,0:T(8,128)(2,1)S(1)} %copy-done.27, bf16[3,4096,512]{2,1,0:T(8,128)(2,1)} %bitcast.174), kind=kOutput, calls=%fused_computation.13 | convolution fusion | flops 536870912 | bytes 5505024 | tf_op jit(solution)/shard_map/dot_general | solution.py:113
  61.7 1.3 copy.41
  63.0 3.5 %all-to-all-start = ((f32[3,128,512]{1,0,2:T(4,128)}), f32[3,128,512]{1,0,2:T(4,128)S(1)}, u32[]{:S(2)}, u32[]{:S(2)}) async-start(f32[3,128,512]{1,0,2:T(4,128)} %copy.41), calls=%async_computation | async-start | bytes 2097152 | tf_op jit(solution)/shard_map/all_to_all | solution.py:85
  66.5 1.8 fusion.133
  68.3 24.5 %all-gather.5.cloned.1.call-done = bf16[128,4096]{1,0:T(8,128)(2,1)} async-done(((bf16[128,512]{1,0:T(8,128)(2,1)}), bf16[128,4096]{1,0:T(8,128)(2,1)}) %all-gather.5.cloned.1.call-update) | async-done | bytes 1048592 | tf_op jit(solution)/shard_map/all_gather | solution.py:110
  92.8 4.5 %fusion.135 = f32[128,512]{0,1:T(8,128)} fusion(bf16[128,4096]{1,0:T(8,128)(2,1)} %all-gather.5.cloned.1.call-done, bf16[512,4096]{1,0:T(8,128)(2,1)} %param.13), kind=kOutput, calls=%fused_computation.178 | convolution fusion | flops 536870912 | bytes 5505024 | tf_op jit(solution)/shard_map/all_to_all | solution.py:85
  97.3 4.0 %all-to-all-start.4 = ((f32[128,4,128]{0,2,1:T(8,128)}), f32[128,4,128]{0,2,1:T(8,128)}, u32[]{:S(2)}, u32[]{:S(2)}) async-start(f32[128,4,128]{0,2,1:T(8,128)} %bitcast.30), calls=%async_computation.4 | async-start | bytes 524288 | tf_op jit(solution)/shard_map/all_to_all | solution.py:85
  101.4 1.8 copy.79
  103.3 0.7 copy.82
  104.6 1.0 fusion.132
  106.2 0.5 fusion.19
  106.7 0.7 copy-done.10
  107.4 1.0 fusion.117
  108.4 0.8 copy-done.13
  109.2 1.2 fusion.64
  110.5 3.3 %fusion.111 = (bf16[16,4,8,128]{3,2,1,0:T(8,128)(2,1)S(1)}, f32[512,128]{0,1:T(8,128)}, f32[512,128]{0,1:T(8,128)}) fusion(f32[512,128]{0,1:T(8,128)} %bitcast.184, f32[128]{0:T(128)S(1)} %get-tuple-element.19, f32[128]{0:T(128)S(1)} %get-tuple-element.20, f32[128]{0:T(128)S(1)} %get-tuple-element.13, f32[512,128]{0,1:T(8,128)S(1)} %get-tuple-element.26, ...), kind=kOutput, calls=%fused_computation.144 | convolution fusion | flops 202375168 | bytes 4065280 | tf_op jit(solution)/shard_map/dot_general | solution.py:25
  113.8 0.7 copy.83
  114.5 3.5 %all-to-all-start.2 = ((bf16[4,128,128]{1,2,0:T(8,128)(2,1)}), bf16[4,128,128]{1,2,0:T(8,128)(2,1)S(1)}, u32[]{:S(2)}, u32[]{:S(2)}) async-start(bf16[4,128,128]{1,2,0:T(8,128)(2,1)} %bitcast.171), calls=%async_computation.2 | async-start | bytes 262144 | tf_op jit(solution)/shard_map/all_to_all | solution.py:89
  118.1 1.5 fusion.112
  119.6 2.0 fusion.119
  121.7 1.6 fusion.57
  123.4 1.5 fusion.129
  125.2 1.0 fusion.115
  127.6 1.1 copy.51
  128.7 3.5 %all-to-all-start.5 = ((bf16[3,512,128]{2,0,1:T(4,128)(2,1)}), bf16[3,512,128]{2,0,1:T(4,128)(2,1)S(1)}, u32[]{:S(2)}, u32[]{:S(2)}) async-start(bf16[3,512,128]{2,0,1:T(4,128)(2,1)} %copy.51), calls=%async_computation.5 | async-start | bytes 1048576 | tf_op jit(solution)/shard_map/all_to_all | solution.py:89
  132.2 2.9 %convolution_convert_fusion = bf16[128,4096]{1,0:T(8,128)(2,1)S(1)} fusion(bf16[128,512]{0,1:T(8,128)(2,1)S(1)} %bitcast.195, bf16[512,4096]{1,0:T(8,128)(2,1)} %param.13), kind=kOutput, calls=%fused_computation.3 | convolution fusion | flops 537395200 | bytes 5373952 | tf_op jit(solution)/shard_map/dot_general | solution.py:123
  135.1 1.1 copy.78
  136.2 4.8 %all-to-all-done.5 = bf16[3,512,128]{2,0,1:T(4,128)(2,1)S(1)} async-done(((bf16[3,512,128]{2,0,1:T(4,128)(2,1)}), bf16[3,512,128]{2,0,1:T(4,128)(2,1)S(1)}, u32[]{:S(2)}, u32[]{:S(2)}) %all-to-all-start.5) | async-done | bytes 393248 | tf_op jit(solution)/shard_map/all_to_all | solution.py:89
  141.0 3.6 %all-to-all-start.3 = ((bf16[8,128,512]{2,1,0:T(8,128)(2,1)}), bf16[8,128,512]{2,1,0:T(8,128)(2,1)S(1)}, u32[]{:S(2)}, u32[]{:S(2)}) async-start(bf16[8,128,512]{2,1,0:T(8,128)(2,1)} %bitcast.166), calls=%async_computation.3 | async-start | bytes 2097152 | tf_op jit(solution)/shard_map/all_to_all | solution.py:96
  145.1 3.7 %fusion.1 = f32[128,4096]{1,0:T(8,128)S(1)} fusion(bf16[128,512]{0,1:T(8,128)(2,1)S(1)} %bitcast.194, bf16[3,4096,512]{2,1,0:T(8,128)(2,1)} %bitcast.175), kind=kOutput, calls=%fused_computation.7 | convolution fusion | flops 536870912 | bytes 6422528 | tf_op jit(solution)/shard_map/dot_general | solution.py:126
  148.8 3.8 %convolution_add_fusion.1 = f32[128,4096]{1,0:T(8,128)S(1)} fusion(f32[128,4096]{1,0:T(8,128)S(1)} %fusion.1, bf16[128,512]{0,1:T(8,128)(2,1)S(1)} %bitcast.193, bf16[3,4096,512]{2,1,0:T(8,128)(2,1)} %bitcast.176), kind=kOutput, calls=%fused_computation.1 | convolution fusion | flops 537395200 | bytes 8519680 | tf_op jit(solution)/shard_map/dot_general | solution.py:126
  152.5 3.7 %fusion = bf16[128,4096]{1,0:T(8,128)(2,1)S(1)} fusion(f32[128,4096]{1,0:T(8,128)S(1)} %convolution_add_fusion.1, bf16[128,512]{0,1:T(8,128)(2,1)S(1)} %bitcast.192, bf16[3,4096,512]{2,1,0:T(8,128)(2,1)} %bitcast.177), kind=kOutput, calls=%fused_computation.2 | convolution fusion | flops 537919488 | bytes 7471104 | tf_op jit(solution)/shard_map/dot_general | solution.py:126
  156.3 1.1 copy.77
  157.4 12.9 %all-to-all-done.3 = bf16[8,128,512]{2,1,0:T(8,128)(2,1)S(1)} async-done(((bf16[8,128,512]{2,1,0:T(8,128)(2,1)}), bf16[8,128,512]{2,1,0:T(8,128)(2,1)S(1)}, u32[]{:S(2)}, u32[]{:S(2)}) %all-to-all-start.3) | async-done | bytes 1048608 | tf_op jit(solution)/shard_map/all_to_all | solution.py:96
  170.3 3.6 %all-to-all-start.6 = ((bf16[8,128,512]{2,1,0:T(8,128)(2,1)}), bf16[8,128,512]{2,1,0:T(8,128)(2,1)S(1)}, u32[]{:S(2)}, u32[]{:S(2)}) async-start(bf16[8,128,512]{2,1,0:T(8,128)(2,1)} %bitcast.164), calls=%async_computation.6 | async-start | bytes 2097152 | tf_op jit(solution)/shard_map/all_to_all | solution.py:96
  173.9 0.8 reduce_sum.24
  174.7 25.1 %all-to-all-done.6 = bf16[8,128,512]{2,1,0:T(8,128)(2,1)S(1)} async-done(((bf16[8,128,512]{2,1,0:T(8,128)(2,1)}), bf16[8,128,512]{2,1,0:T(8,128)(2,1)S(1)}, u32[]{:S(2)}, u32[]{:S(2)}) %all-to-all-start.6) | async-done | bytes 1048608 | tf_op jit(solution)/shard_map/all_to_all | solution.py:96
  199.9 0.8 reduce_sum.25
  (81 shorter events, 3.7 us)
Async XLA Ops:
  7.2 7.8 %copy-start = (f32[2,512]{1,0:T(2,128)S(1)}, f32[2,512]{1,0:T(2,128)}, u32[]{:S(2)}) copy-start(f32[2,512]{1,0:T(2,128)} %param.12) | copy-start | bytes 12292
  7.2 16.2 %copy-start.1 = (f32[1024,512]{1,0:T(8,128)S(1)}, f32[1024,512]{1,0:T(8,128)}, u32[]{:S(2)}) copy-start(f32[1024,512]{1,0:T(8,128)} %constant.21.clone) | copy-start | bytes 6291460
  7.2 45.1 %all-gather.3.cloned.1.call-start = ((), (), s32[]{:S(2)}) async-start(), calls=%async_computation.7 | async-start | bytes 1179648 | tf_op jit(solution)/shard_map/all_gather | solution.py:109
  10.0 13.1 %all-to-all-start.1 = ((f32[2,128,512]{1,0,2:T(2,128)}), f32[2,128,512]{1,0,2:T(2,128)S(1)}, u32[]{:S(2)}, u32[]{:S(2)}) async-start(f32[2,128,512]{1,0,2:T(2,128)} %copy.43), calls=%async_computation.1 | async-start | bytes 1048576 | tf_op jit(solution)/shard_map/all_to_all | solution.py:85
  14.2 78.6 %all-gather.5.cloned.1.call-start = ((), (), s32[]{:S(2)}) async-start(), calls=%async_computation.8 | async-start | bytes 1179648 | tf_op jit(solution)/shard_map/all_gather | solution.py:110
  15.9 88.2 %copy-start.14 = (f32[128]{0:T(128)}, f32[128]{0:T(128)S(1)}, u32[]{:S(2)}) copy-start(f32[128]{0:T(128)S(1)} %get-tuple-element.16) | copy-start | bytes 1540
  15.9 88.2 %copy-start.16 = (f32[128]{0:T(128)}, f32[128]{0:T(128)S(1)}, u32[]{:S(2)}) copy-start(f32[128]{0:T(128)S(1)} %get-tuple-element.17) | copy-start | bytes 1540
  15.9 88.2 %copy-start.18 = (f32[128]{0:T(128)}, f32[128]{0:T(128)S(1)}, u32[]{:S(2)}) copy-start(f32[128]{0:T(128)S(1)} %get-tuple-element.18) | copy-start | bytes 1540
  15.9 94.5 %copy-start.20 = (f32[128]{0:T(128)}, f32[128]{0:T(128)S(1)}, u32[]{:S(2)}) copy-start(f32[128]{0:T(128)S(1)} %get-tuple-element.13) | copy-start | bytes 1540
  15.9 94.5 %copy-start.21 = (f32[128]{0:T(128)}, f32[128]{0:T(128)S(1)}, u32[]{:S(2)}) copy-start(f32[128]{0:T(128)S(1)} %get-tuple-element.19) | copy-start | bytes 1540
  15.9 94.5 %copy-start.22 = (f32[128]{0:T(128)}, f32[128]{0:T(128)S(1)}, u32[]{:S(2)}) copy-start(f32[128]{0:T(128)S(1)} %get-tuple-element.20) | copy-start | bytes 1540
  16.0 90.2 %copy-start.23 = (f32[128]{0:T(128)}, f32[128]{0:T(128)S(1)}, u32[]{:S(2)}) copy-start(f32[128]{0:T(128)S(1)} %get-tuple-element.23) | copy-start | bytes 1540
  16.0 94.5 %copy-start.25 = (f32[128]{0:T(128)}, f32[128]{0:T(128)S(1)}, u32[]{:S(2)}) copy-start(f32[128]{0:T(128)S(1)} %get-tuple-element.22) | copy-start | bytes 1540
  52.3 3.3 %copy-start.27 = (bf16[128,4096]{1,0:T(8,128)(2,1)S(1)}, bf16[128,4096]{1,0:T(8,128)(2,1)}, u32[]{:S(2)}) copy-start(bf16[128,4096]{1,0:T(8,128)(2,1)} %all-gather.3.cloned.1.call-done) | copy-start | bytes 3145732
  63.0 34.3 %all-to-all-start = ((f32[3,128,512]{1,0,2:T(4,128)}), f32[3,128,512]{1,0,2:T(4,128)S(1)}, u32[]{:S(2)}, u32[]{:S(2)}) async-start(f32[3,128,512]{1,0,2:T(4,128)} %copy.41), calls=%async_computation | async-start | bytes 2097152 | tf_op jit(solution)/shard_map/all_to_all | solution.py:85
  97.3 4.1 %copy-start.9 = (f32[3,128,512]{1,0,2:T(4,128)}, f32[3,128,512]{1,0,2:T(4,128)S(1)}, u32[]{:S(2)}) copy-start(f32[3,128,512]{1,0,2:T(4,128)S(1)} %all-to-all-done) | copy-start | bytes 2359300
  97.3 13.1 %all-to-all-start.4 = ((f32[128,4,128]{0,2,1:T(8,128)}), f32[128,4,128]{0,2,1:T(8,128)}, u32[]{:S(2)}, u32[]{:S(2)}) async-start(f32[128,4,128]{0,2,1:T(8,128)} %bitcast.30), calls=%async_computation.4 | async-start | bytes 524288 | tf_op jit(solution)/shard_map/all_to_all | solution.py:85
  101.4 4.2 %copy-start.2 = (f32[512,512]{1,0:T(8,128)S(1)}, f32[512,512]{1,0:T(8,128)}, u32[]{:S(2)}) copy-start(f32[512,512]{1,0:T(8,128)} %constant.46) | copy-start | bytes 3145732
  101.4 4.2 %copy-start.7 = (f32[1024,128]{1,0:T(8,128)S(1)}, f32[1024,128]{1,0:T(8,128)}, u32[]{:S(2)}) copy-start(f32[1024,128]{1,0:T(8,128)} %fusion.133) | copy-start | bytes 1572868
  103.3 2.9 %copy-start.3 = (f32[512,512]{1,0:T(8,128)S(1)}, f32[512,512]{1,0:T(8,128)}, u32[]{:S(2)}) copy-start(f32[512,512]{1,0:T(8,128)} %constant.47) | copy-start | bytes 3145732
  105.6 3.6 %copy-start.5 = (f32[1024,128]{1,0:T(8,128)S(1)}, f32[1024,128]{1,0:T(8,128)}, u32[]{:S(2)}) copy-start(f32[1024,128]{1,0:T(8,128)} %fusion.134) | copy-start | bytes 1572868
  106.7 0.7 copy-start.10
  108.4 0.8 copy-start.13
  114.5 14.2 %all-to-all-start.2 = ((bf16[4,128,128]{1,2,0:T(8,128)(2,1)}), bf16[4,128,128]{1,2,0:T(8,128)(2,1)S(1)}, u32[]{:S(2)}, u32[]{:S(2)}) async-start(bf16[4,128,128]{1,2,0:T(8,128)(2,1)} %bitcast.171), calls=%async_computation.2 | async-start | bytes 262144 | tf_op jit(solution)/shard_map/all_to_all | solution.py:89
  118.0 5.3 %copy-start.4 = (f32[512,512]{1,0:T(8,128)S(1)}, f32[512,512]{1,0:T(8,128)}, u32[]{:S(2)}) copy-start(f32[512,512]{1,0:T(8,128)} %constant.47) | copy-start | bytes 3145732
  118.0 5.3 %copy-start.6 = (f32[1024,128]{1,0:T(8,128)S(1)}, f32[1024,128]{1,0:T(8,128)}, u32[]{:S(2)}) copy-start(f32[1024,128]{1,0:T(8,128)} %fusion.134) | copy-start | bytes 1572868
  118.0 5.3 %copy-start.11 = (f32[512,128]{0,1:T(8,128)S(1)}, f32[512,128]{0,1:T(8,128)}, u32[]{:S(2)}) copy-start(f32[512,128]{0,1:T(8,128)} %copy-done.10) | copy-start | bytes 786436
  118.1 5.3 %copy-start.12 = (f32[512,128]{0,1:T(8,128)S(1)}, f32[512,128]{0,1:T(8,128)}, u32[]{:S(2)}) copy-start(f32[512,128]{0,1:T(8,128)} %get-tuple-element.3) | copy-start | bytes 786436
  118.1 5.3 %copy-start.26 = (f32[128]{0:T(128)S(1)}, f32[128]{0:T(128)}, u32[]{:S(2)}) copy-start(f32[128]{0:T(128)} %copy-done.25) | copy-start | bytes 1540
  118.1 6.8 %copy-start.15 = (f32[128]{0:T(128)S(1)}, f32[128]{0:T(128)}, u32[]{:S(2)}) copy-start(f32[128]{0:T(128)} %copy-done.14) | copy-start | bytes 1540
  118.1 6.8 %copy-start.17 = (f32[128]{0:T(128)S(1)}, f32[128]{0:T(128)}, u32[]{:S(2)}) copy-start(f32[128]{0:T(128)} %copy-done.16) | copy-start | bytes 1540
  118.1 6.8 %copy-start.19 = (f32[128]{0:T(128)S(1)}, f32[128]{0:T(128)}, u32[]{:S(2)}) copy-start(f32[128]{0:T(128)} %copy-done.18) | copy-start | bytes 1540
  121.7 4.5 %copy-start.8 = (f32[1024,128]{1,0:T(8,128)S(1)}, f32[1024,128]{1,0:T(8,128)}, u32[]{:S(2)}) copy-start(f32[1024,128]{1,0:T(8,128)} %fusion.133) | copy-start | bytes 1572868
  123.4 3.4 %copy-start.24 = (f32[128]{0:T(128)S(1)}, f32[128]{0:T(128)}, u32[]{:S(2)}) copy-start(f32[128]{0:T(128)} %copy-done.23) | copy-start | bytes 1540
  128.7 12.3 %all-to-all-start.5 = ((bf16[3,512,128]{2,0,1:T(4,128)(2,1)}), bf16[3,512,128]{2,0,1:T(4,128)(2,1)S(1)}, u32[]{:S(2)}, u32[]{:S(2)}) async-start(bf16[3,512,128]{2,0,1:T(4,128)(2,1)} %copy.51), calls=%async_computation.5 | async-start | bytes 1048576 | tf_op jit(solution)/shard_map/all_to_all | solution.py:89
  141.0 29.3 %all-to-all-start.3 = ((bf16[8,128,512]{2,1,0:T(8,128)(2,1)}), bf16[8,128,512]{2,1,0:T(8,128)(2,1)S(1)}, u32[]{:S(2)}, u32[]{:S(2)}) async-start(bf16[8,128,512]{2,1,0:T(8,128)(2,1)} %bitcast.166), calls=%async_computation.3 | async-start | bytes 2097152 | tf_op jit(solution)/shard_map/all_to_all | solution.py:96
  170.3 29.6 %all-to-all-start.6 = ((bf16[8,128,512]{2,1,0:T(8,128)(2,1)}), bf16[8,128,512]{2,1,0:T(8,128)(2,1)S(1)}, u32[]{:S(2)}, u32[]{:S(2)}) async-start(bf16[8,128,512]{2,1,0:T(8,128)(2,1)} %bitcast.164), calls=%async_computation.6 | async-start | bytes 2097152 | tf_op jit(solution)/shard_map/all_to_all | solution.py:96
Sparse Core Ops, SparseCore 0:
  10.1 42.2 all-gather.2
  54.4 38.4 all-gather.4

commit v2 on v1

--- a/solution.py
+++ b/solution.py
@@ -1,9 +1,12 @@
+import functools
 import math
 
 import jax
 import jax.numpy as jnp
 import numpy as np
 from jax import lax
+from jax.experimental import pallas as pl
+from jax.experimental.pallas import tpu as pltpu
 from jax.sharding import PartitionSpec as P
 
 FINE = lax.Precision.HIGH
@@ -97,6 +100,166 @@
     return jnp.sum(got.astype(jnp.float32), axis=0).astype(jnp.bfloat16)
 
 
+MESH = pl.DeviceIdType.MESH
+
+
+def greet(chan_peers, seq_peers):
+    barrier = pltpu.get_barrier_semaphore()
+    for axis, peers in (("chan", chan_peers), ("seq", seq_peers)):
+        for peer in peers:
+            pl.semaphore_signal(barrier, inc=1, device_id={axis: peer}, device_id_type=MESH)
+    pl.semaphore_wait(barrier, len(chan_peers) + len(seq_peers))
+
+
+def project_kernel(
+    chan_count, seq_count, tok, cot, w, ow, out,
+    tok_all, cot_all, w_all, ow_all, acc, grad,
+    w_sem, send_sem, recv_sem, seq_send, seq_recv, own_sem,
+):
+    me, row = lax.axis_index("chan"), lax.axis_index("seq")
+    outer_count = chan_count // 2
+    outer, inner = me // 2, lax.rem(me, 2)
+    partner = outer * 2 + 1 - inner
+    depth = tok.shape[1]
+    part = out.shape[3]
+    loads = [pltpu.make_async_copy(w.at[j], w_all.at[j], w_sem.at[j]) for j in range(3)]
+    loads.append(pltpu.make_async_copy(ow, ow_all, w_sem.at[3]))
+    for load in loads:
+        load.start()
+
+    def column(k, side):
+        return lax.rem(outer + k + outer_count, outer_count) * 2 + side
+
+    def seq_peer(k):
+        return lax.rem(row + k, seq_count)
+
+    chan_peers = [partner] + [column(k, inner) for k in range(1, outer_count)]
+    greet(chan_peers, [seq_peer(k) for k in range(1, seq_count)])
+
+    def push(which, source, target, owner, slot):
+        place = (tok_all, cot_all)[which].at[owner]
+        return pltpu.make_async_remote_copy(
+            src_ref=source,
+            dst_ref=place,
+            send_sem=send_sem.at[which, slot],
+            recv_sem=recv_sem.at[which, slot],
+            device_id={"chan": target},
+            device_id_type=MESH,
+        )
+
+    held = [{}, {}]
+    for which, source in enumerate((tok, cot)):
+        for k in range(1, outer_count):
+            held[which][k] = push(which, source, column(k, inner), me, k)
+        held[which][0] = push(which, source, partner, me, 0)
+        for copy in held[which].values():
+            copy.start()
+
+    def pass_on(which, k):
+        held[which][k].wait_recv()
+        owner = column(-k, inner)
+        slot = outer_count - 1 + k
+        held[which][slot] = push(which, (tok_all, cot_all)[which].at[owner], partner, owner, slot)
+        held[which][slot].start()
+        return owner
+
+    def add_tok(block, owner, first=False):
+        lines = pl.ds(pl.multiple_of(owner * depth, depth), depth)
+        for j in range(3):
+            product = jnp.dot(block, w_all[j, lines, :], preferred_element_type=jnp.float32)
+            acc[j] = product if first else acc[j] + product
+
+    def add_cot(block, owner, first=False):
+        lines = pl.ds(pl.multiple_of(owner * depth, depth), depth)
+        product = lax.dot_general(
+            block, ow_all[:, lines], (((1,), (1,)), ((), ())), preferred_element_type=jnp.float32
+        )
+        grad[0] = product if first else grad[0] + product
+
+    for load in loads[:3]:
+        load.wait()
+    add_tok(tok[...], me, True)
+    for k in range(1, outer_count):
+        owner = pass_on(0, k)
+        add_tok(tok_all[owner], owner)
+    held[0][0].wait_recv()
+    add_tok(tok_all[partner], partner)
+    loads[3].wait()
+    add_cot(cot[...], me, True)
+    for k in range(1, outer_count):
+        owner = pass_on(1, k)
+        add_cot(cot_all[owner], owner)
+        held[0][outer_count - 1 + k].wait_recv()
+        owner = column(-k, 1 - inner)
+        add_tok(tok_all[owner], owner)
+
+    def spread(source, slots, where):
+        copies = []
+        for k in range(1, seq_count):
+            peer = seq_peer(k)
+            lanes = pl.ds(pl.multiple_of(peer * part, part), part)
+            copies.append(
+                pltpu.make_async_remote_copy(
+                    src_ref=source.at[:, :, lanes],
+                    dst_ref=out.at[slots, row],
+                    send_sem=seq_send.at[where, k],
+                    recv_sem=seq_recv.at[where, k],
+                    device_id={"seq": peer},
+                    device_id_type=MESH,
+                )
+            )
+        lanes = pl.ds(pl.multiple_of(row * part, part), part)
+        own = pltpu.make_async_copy(source.at[:, :, lanes], out.at[slots, row], own_sem.at[where])
+        for copy in copies + [own]:
+            copy.start()
+        return copies + [own]
+
+    last = spread(acc, pl.ds(0, 3), 0)
+    held[1][0].wait_recv()
+    add_cot(cot_all[partner], partner)
+    for k in range(1, outer_count):
+        held[1][outer_count - 1 + k].wait_recv()
+        owner = column(-k, 1 - inner)
+        add_cot(cot_all[owner], owner)
+    last = last + spread(grad, pl.ds(3, 1), 1)
+    for copies in held:
+        for copy in copies.values():
+            copy.wait_send()
+    for copy in last:
+        copy.wait()
+
+
+def project(tokens, cotangent, weights, out_weight):
+    chan_count, seq_count = lax.axis_size("chan"), lax.axis_size("seq")
+    rows, depth = tokens.shape
+    chans = weights.shape[2]
+    vmem = pl.BlockSpec(memory_space=pltpu.VMEM)
+    anywhere = pl.BlockSpec(memory_space=pl.ANY)
+    return pl.pallas_call(
+        functools.partial(project_kernel, chan_count, seq_count),
+        out_shape=jax.ShapeDtypeStruct((4, seq_count, rows, chans // seq_count), jnp.float32),
+        in_specs=[vmem, vmem, anywhere, anywhere],
+        out_specs=vmem,
+        scratch_shapes=[
+            pltpu.VMEM((chan_count, rows, depth), jnp.bfloat16),
+            pltpu.VMEM((chan_count, rows, depth), jnp.bfloat16),
+            pltpu.VMEM(weights.shape, jnp.bfloat16),
+            pltpu.VMEM(out_weight.shape, jnp.bfloat16),
+            pltpu.VMEM((3, rows, chans), jnp.float32),
+            pltpu.VMEM((1, rows, chans), jnp.float32),
+            pltpu.SemaphoreType.DMA((4,)),
+            pltpu.SemaphoreType.DMA((2, chan_count)),
+            pltpu.SemaphoreType.DMA((2, chan_count)),
+            pltpu.SemaphoreType.DMA((2, seq_count)),
+            pltpu.SemaphoreType.DMA((2, seq_count)),
+            pltpu.SemaphoreType.DMA((2,)),
+        ],
+        compiler_params=pltpu.CompilerParams(
+            collective_id=0, has_side_effects=True, vmem_limit_bytes=40 * 2**20
+        ),
+    )(tokens, cotangent, weights, out_weight)
+
+
 def on_device(tokens, in_weight, short_kernel, filters, skip_gain, out_weight, cotangent):
     seq_count = lax.axis_size("seq")
     chans = in_weight.shape[2]
@@ -106,17 +269,22 @@
     table = jnp.asarray(odd_table(tokens.shape[0] * seq_count))
     taps = lax.dynamic_slice_in_dim(short_kernel, start, part, 2)
     skip = lax.dynamic_slice_in_dim(skip_gain, start, part, 1)
-    rows = lax.all_gather(tokens, "chan", axis=1, tiled=True)
-    grad_rows = lax.all_gather(cotangent, "chan", axis=1, tiled=True)
     local_filters = swap_in(filters)
-    projected = jnp.stack(
-        [jnp.dot(rows, weights[j], preferred_element_type=jnp.float32) for j in range(3)]
-    )
-    grad_two = lax.dot_general(
-        grad_rows, out_weight, (((1,), (1,)), ((), ())), preferred_element_type=jnp.float32
-    )
-    projected = swap_in(projected)
-    grad_two = swap_in(grad_two)
+    if part % 128 == 0 and tokens.shape[0] % 16 == 0 and lax.axis_size("chan") % 2 == 0:
+        both = project(tokens, cotangent, weights, out_weight)
+        both = both.reshape(4, seq_count * tokens.shape[0], part)
+        projected, grad_two = both[:3], both[3]
+    else:
+        rows = lax.all_gather(tokens, "chan", axis=1, tiled=True)
+        grad_rows = lax.all_gather(cotangent, "chan", axis=1, tiled=True)
+        projected = jnp.stack(
+            [jnp.dot(rows, weights[j], preferred_element_type=jnp.float32) for j in range(3)]
+        )
+        grad_two = lax.dot_general(
+            grad_rows, out_weight, (((1,), (1,)), ((), ())), preferred_element_type=jnp.float32
+        )
+        projected = swap_in(projected)
+        grad_two = swap_in(grad_two)
     second_out, grads = middle(projected, grad_two, taps, local_filters, skip, table)
     second_out = swap_out(second_out)
     grads = swap_out(grads)

time: 209 us -> 159 us (0.76)
  waiting for transfers between devices: 103 us -> 42.7 us
  Pallas kernels: 0 us -> 39.8 us
  matrix products: 46.3 us -> 29.1 us
  between operations: 14.7 us -> 1.3 us
  local copies, waits for them, and re-layouts: 13.3 us -> 18.2 us
  starting transfers between devices: 26 us -> 22.1 us
    all_gather x2 -> x0, waiting for transfers between devices: 51.6 us -> none  [the longest x1 27.1 us: on_device(): rows = lax.all_gather(tokens, 'chan', axis=1, tiled=True)]
    pallas_call x0 -> x1, Pallas kernels: none -> 39.8 us  [project(): pl.pallas_call(functools.partial(project_kernel, chan_count, seq_count),...]
    dot_general x3 -> x0, matrix products: 9.26 us -> none  [on_device(): jnp.dot(rows, weights[j], preferred_element_type=jnp.float32)]
    all_to_all x3 -> x1, starting transfers between devices: 11.8 us -> 4.24 us  [swap_in(): lax.all_to_all(array, 'seq', array.ndim - 1, array.ndim - 2, tiled=True)]
    all_to_all x3 -> x1, waiting for transfers between devices: 7.08 us -> 0.01 us  [swap_in(): lax.all_to_all(array, 'seq', array.ndim - 1, array.ndim - 2, tiled=True)]
    dot_general x8, matrix products: 9.78 us -> 5.06 us  [inverse(): lax.dot_general(table, spec, (((0,), (0,)), ((), ())), precision=FINE)]
    squeeze x0 -> x4, local copies, waits for them, and re-layouts: none -> 4.63 us  [the longest x3 2.77 us: middle(): total = taps[0, j] * projected[j]]
    all_to_all x1 -> x0, matrix products: 4.47 us -> none  [swap_in(): lax.all_to_all(array, 'seq', array.ndim - 1, array.ndim - 2, tiled=True)]
  transfers between devices with their start and end apart: 9 -> 5, of which waited for: 6 -> 3; matrix products, arithmetic and copies ran while one was open for 28% -> 23% of each run, Pallas kernels for 0% -> 25%
where the time goes in v2:
time: 159 us; the launch traced here: 158 us
  waiting for transfers between devices  42.7 us (27%)
  Pallas kernels  39.8 us (25%)
  matrix products  29.1 us (18%)
  starting transfers between devices  22.1 us (14%)
  local copies, waits for them, and re-layouts  18.2 us (11%)
  other arithmetic  5.33 us (3%)
    pallas_call x1, Pallas kernels, project(): pl.pallas_call(functools.partial(project_kernel, chan_count, seq_count),...  39.8 us
    all_to_all x2, waiting for transfers between devices, share(): got = lax.all_to_all(sent, 'chan', 0, 0, tiled=True)  37.9 us
    dot_general x3, matrix products, on_device(): lax.dot_general(grads[j], weights[j], (((1,), (1,)), ((), ())), preferred...  11.2 us
    all_to_all x2, starting transfers between devices, share(): got = lax.all_to_all(sent, 'chan', 0, 0, tiled=True)  10.9 us
    dot_general x6, matrix products, forward(): return jnp.dot(table, signal, precision=FINE)  9.86 us
    all_to_all x2, starting transfers between devices, swap_out(): lax.all_to_all(array, 'seq', array.ndim - 2, array.ndim - 1, tiled=True)  6.98 us
    dot_general x8, matrix products, inverse(): lax.dot_general(table, spec, (((0,), (0,)), ((), ())), precision=FINE)  5.06 us
    all_to_all x2, waiting for transfers between devices, swap_out(): lax.all_to_all(array, 'seq', array.ndim - 2, array.ndim - 1, tiled=True)  4.76 us
  transfers between devices with their start and end apart: 5, of which 3 were waited for; matrix products, arithmetic and copies ran while one was open for 23% of the time, Pallas kernels for 25%

profile of v2, /device:TPU:0, one launch (start us, length us, event | category | flops | bytes accessed | tf_op | source)
XLA Modules:
  0.0 158.5 jit_solution(9076505245970440858)
XLA Ops:
  0.7 2.1 %copy.78 = f32[2,128,512]{1,0,2:T(2,128)} copy(f32[2,128,512]{2,1,0:T(8,128)} %param.11) | data formatting | bytes 1048576 | tf_op args[3]
  2.8 4.2 %all-to-all-start = ((f32[2,128,512]{1,0,2:T(2,128)}), f32[2,128,512]{1,0,2:T(2,128)S(1)}, u32[]{:S(2)}, u32[]{:S(2)}) async-start(f32[2,128,512]{1,0,2:T(2,128)} %copy.78), calls=%async_computation | async-start | bytes 1048576 | tf_op jit(solution)/shard_map/all_to_all | solution.py:88
  7.0 2.2 %copy-done.1 = bf16[512,4096]{1,0:T(8,128)(2,1)S(1)} copy-done((bf16[512,4096]{1,0:T(8,128)(2,1)S(1)}, bf16[512,4096]{1,0:T(8,128)(2,1)}, u32[]{:S(2)}) %copy-start.1) | copy-done | bytes 4194328
  9.2 39.8 %shard_map.95 = f32[4,4,128,128]{3,2,1,0:T(8,128)S(1)} custom-call(bf16[128,512]{1,0:T(8,128)(2,1)S(1)} %copy-done.2, bf16[128,512]{1,0:T(8,128)(2,1)S(1)} %copy-done.3, bf16[3,4096,512]{2,1,0:T(8,128)(2,1)} %bitcast.115, bf16[512,4096]{1,0:T(8,128)(2,1)S(1)} %copy-done.1), custom_call_target="tpu_custom_call" | custom-call | tf_op jit(solution)/shard_map/pallas_call | solution.py:238
  49.0 0.9 fusion.121
  50.1 0.9 copy.72
  50.9 0.9 fusion.116
  51.9 1.7 %fusion.20 = (f32[512,128]{0,1:T(8,128)S(1)}, f32[512,128]{0,1:T(8,128)S(1)}) fusion(f32[512,128]{0,1:T(8,128)} %copy.72, f32[128]{0:T(128)S(1)} %get-tuple-element.17, f32[128]{0:T(128)S(1)} %get-tuple-element.18, f32[128]{0:T(128)S(1)} %get-tuple-element.19, f32[512,128]{0,1:T(8,128)S(1)} %copy.75, f32[128]{0:T(128)S(1)} %get-tuple-element.22, ...), kind=kLoop, calls=%fused_computation.45 | loop fusion | flops 655360 | bytes 1051648 | tf_op jit(solution)/shard_map/add | solution.py:55
  53.6 1.9 %copy.84 = f32[512,128]{0,1:T(8,128)} copy(f32[512,128]{1,0:T(8,128)} %bitcast.124) | data formatting | bytes 524288 | tf_op jit(solution)/shard_map/squeeze | solution.py:276
  55.5 1.8 %copy.69 = f32[512,128]{0,1:T(8,128)} copy(f32[512,128]{1,0:T(8,128)} %bitcast.123) | data formatting | bytes 524288 | tf_op jit(solution)/shard_map/squeeze | solution.py:53
  57.3 1.8 %fusion.127 = f32[1024,128]{1,0:T(8,128)} fusion(f32[1024,512]{1,0:T(8,128)S(1)} %copy-done.4, f32[512,128]{0,1:T(8,128)S(1)} %get-tuple-element.28), kind=kOutput, calls=%fused_computation.163 | convolution fusion | flops 402653184 | bytes 2883584 | tf_op jit(solution)/shard_map/dot_general | solution.py:23
  59.1 0.8 fusion.122
  60.0 1.8 %fusion.129 = f32[1024,128]{1,0:T(8,128)} fusion(f32[1024,512]{1,0:T(8,128)S(1)} %copy-done.4, f32[512,128]{1,0:T(8,128)S(1)} %bitcast.127), kind=kOutput, calls=%fused_computation.165 | convolution fusion | flops 402653184 | bytes 2883584 | tf_op jit(solution)/shard_map/dot_general | solution.py:23
  61.9 1.9 %copy.80 = f32[1,4,128,128]{3,2,1,0:T(8,128)} copy(f32[1,4,128,128]{2,3,1,0:T(8,128)} %get-tuple-element.9) | data formatting | bytes 524288 | tf_op jit(solution)/shard_map/slice | solution.py:58
  63.8 2.1 %fusion.128 = f32[1024,128]{1,0:T(8,128)S(1)} fusion(f32[1024,512]{1,0:T(8,128)S(1)} %copy-done.4, f32[512,128]{1,0:T(8,128)} %bitcast.128), kind=kOutput, calls=%fused_computation.164 | convolution fusion | flops 402653184 | bytes 2883584 | tf_op jit(solution)/shard_map/dot_general | solution.py:23
  65.9 0.5 fusion.65
  66.4 0.5 fusion.13
  67.0 1.0 fusion.113
  68.1 0.5 fusion.58
  68.7 1.4 fusion.105
  70.1 0.7 copy.100
  70.8 3.5 %all-to-all-start.1 = ((bf16[4,128,128]{1,2,0:T(8,128)(2,1)}), bf16[4,128,128]{1,2,0:T(8,128)(2,1)S(1)}, u32[]{:S(2)}, u32[]{:S(2)}) async-start(bf16[4,128,128]{1,2,0:T(8,128)(2,1)} %bitcast.114), calls=%async_computation.1 | async-start | bytes 262144 | tf_op jit(solution)/shard_map/all_to_all | solution.py:92
  74.3 1.4 fusion.106
  75.8 2.2 %fusion.111 = f32[1024,128]{1,0:T(8,128)S(1)} fusion(f32[1024,512]{1,0:T(8,128)S(1)} %copy-done.4, f32[512,128]{0,1:T(8,128)} %copy.84, f32[512,128]{0,1:T(8,128)} %get-tuple-element.3), kind=kOutput, calls=%fused_computation.138 | convolution fusion | flops 402718720 | bytes 3145728 | tf_op jit(solution)/shard_map/dot_general | solution.py:23
  78.0 0.5 fusion.51
  78.6 0.5 fusion.124
  79.2 0.3 fusion.107
  79.5 1.0 fusion.109
  80.5 0.5 fusion.44
  81.0 0.5 fusion.4
  81.5 0.3 fusion.108
  81.9 1.1 copy.86
  82.9 3.5 %all-to-all-start.3 = ((bf16[3,512,128]{2,0,1:T(4,128)(2,1)}), bf16[3,512,128]{2,0,1:T(4,128)(2,1)S(1)}, u32[]{:S(2)}, u32[]{:S(2)}) async-start(bf16[3,512,128]{2,0,1:T(4,128)(2,1)} %copy.86), calls=%async_computation.3 | async-start | bytes 1048576 | tf_op jit(solution)/shard_map/all_to_all | solution.py:92
  86.4 2.9 %convolution_convert_fusion = bf16[128,4096]{1,0:T(8,128)(2,1)S(1)} fusion(bf16[128,512]{0,1:T(8,128)(2,1)S(1)} %bitcast.132, bf16[512,4096]{1,0:T(8,128)(2,1)} %ow.1), kind=kOutput, calls=%fused_computation.3 | convolution fusion | flops 537395200 | bytes 5373952 | tf_op jit(solution)/shard_map/dot_general | solution.py:291
  89.3 1.1 copy.99
  90.5 4.8 %all-to-all-done.3 = bf16[3,512,128]{2,0,1:T(4,128)(2,1)S(1)} async-done(((bf16[3,512,128]{2,0,1:T(4,128)(2,1)}), bf16[3,512,128]{2,0,1:T(4,128)(2,1)S(1)}, u32[]{:S(2)}, u32[]{:S(2)}) %all-to-all-start.3) | async-done | bytes 393248 | tf_op jit(solution)/shard_map/all_to_all | solution.py:92
  95.2 7.3 %all-to-all-start.2 = ((bf16[8,128,512]{2,1,0:T(8,128)(2,1)}), bf16[8,128,512]{2,1,0:T(8,128)(2,1)S(1)}, u32[]{:S(2)}, u32[]{:S(2)}) async-start(bf16[8,128,512]{2,1,0:T(8,128)(2,1)} %bitcast.113), calls=%async_computation.2 | async-start | bytes 2097152 | tf_op jit(solution)/shard_map/all_to_all | solution.py:99
  102.8 0.1 copy.89
  102.9 0.1 copy.88
  103.0 3.7 %fusion.1 = f32[128,4096]{1,0:T(8,128)S(1)} fusion(bf16[128,512]{0,1:T(8,128)(2,1)S(1)} %bitcast.131, bf16[3,4096,512]{2,1,0:T(8,128)(2,1)} %bitcast.116), kind=kOutput, calls=%fused_computation.7 | convolution fusion | flops 536870912 | bytes 6422528 | tf_op jit(solution)/shard_map/dot_general | solution.py:294
  106.8 3.8 %convolution_add_fusion.1 = f32[128,4096]{1,0:T(8,128)S(1)} fusion(f32[128,4096]{1,0:T(8,128)S(1)} %fusion.1, bf16[128,512]{0,1:T(8,128)(2,1)S(1)} %bitcast.130, bf16[3,4096,512]{2,1,0:T(8,128)(2,1)} %bitcast.117), kind=kOutput, calls=%fused_computation.1 | convolution fusion | flops 537395200 | bytes 8519680 | tf_op jit(solution)/shard_map/dot_general | solution.py:294
  110.5 3.7 %fusion = bf16[128,4096]{1,0:T(8,128)(2,1)S(1)} fusion(f32[128,4096]{1,0:T(8,128)S(1)} %convolution_add_fusion.1, bf16[128,512]{0,1:T(8,128)(2,1)S(1)} %bitcast.129, bf16[3,4096,512]{2,1,0:T(8,128)(2,1)} %bitcast.118), kind=kOutput, calls=%fused_computation.2 | convolution fusion | flops 537919488 | bytes 7471104 | tf_op jit(solution)/shard_map/dot_general | solution.py:294
  114.3 1.1 copy.98
  115.4 12.8 %all-to-all-done.2 = bf16[8,128,512]{2,1,0:T(8,128)(2,1)S(1)} async-done(((bf16[8,128,512]{2,1,0:T(8,128)(2,1)}), bf16[8,128,512]{2,1,0:T(8,128)(2,1)S(1)}, u32[]{:S(2)}, u32[]{:S(2)}) %all-to-all-start.2) | async-done | bytes 1048608 | tf_op jit(solution)/shard_map/all_to_all | solution.py:99
  128.2 3.6 %all-to-all-start.4 = ((bf16[8,128,512]{2,1,0:T(8,128)(2,1)}), bf16[8,128,512]{2,1,0:T(8,128)(2,1)S(1)}, u32[]{:S(2)}, u32[]{:S(2)}) async-start(bf16[8,128,512]{2,1,0:T(8,128)(2,1)} %bitcast.111), calls=%async_computation.4 | async-start | bytes 2097152 | tf_op jit(solution)/shard_map/all_to_all | solution.py:99
  131.8 0.8 reduce_sum.24
  132.6 25.1 %all-to-all-done.4 = bf16[8,128,512]{2,1,0:T(8,128)(2,1)S(1)} async-done(((bf16[8,128,512]{2,1,0:T(8,128)(2,1)}), bf16[8,128,512]{2,1,0:T(8,128)(2,1)S(1)}, u32[]{:S(2)}, u32[]{:S(2)}) %all-to-all-start.4) | async-done | bytes 1048608 | tf_op jit(solution)/shard_map/all_to_all | solution.py:99
  157.6 0.8 reduce_sum.25
  (78 shorter events, 0.8 us)
Async XLA Ops:
  0.6 50.3 %copy-start = (f32[2,512]{1,0:T(2,128)S(1)}, f32[2,512]{1,0:T(2,128)}, u32[]{:S(2)}) copy-start(f32[2,512]{1,0:T(2,128)} %param.12) | copy-start | bytes 12292
  0.6 6.3 %copy-start.3 = (bf16[128,512]{1,0:T(8,128)(2,1)S(1)}, bf16[128,512]{1,0:T(8,128)(2,1)}, u32[]{:S(2)}) copy-start(bf16[128,512]{1,0:T(8,128)(2,1)} %cot.1) | copy-start | bytes 393220
  0.7 6.3 %copy-start.2 = (bf16[128,512]{1,0:T(8,128)(2,1)S(1)}, bf16[128,512]{1,0:T(8,128)(2,1)}, u32[]{:S(2)}) copy-start(bf16[128,512]{1,0:T(8,128)(2,1)} %tok.1) | copy-start | bytes 393220
  2.8 56.3 %all-to-all-start = ((f32[2,128,512]{1,0,2:T(2,128)}), f32[2,128,512]{1,0,2:T(2,128)S(1)}, u32[]{:S(2)}, u32[]{:S(2)}) async-start(f32[2,128,512]{1,0,2:T(2,128)} %copy.78), calls=%async_computation | async-start | bytes 1048576 | tf_op jit(solution)/shard_map/all_to_all | solution.py:88
  7.0 2.2 %copy-start.1 = (bf16[512,4096]{1,0:T(8,128)(2,1)S(1)}, bf16[512,4096]{1,0:T(8,128)(2,1)}, u32[]{:S(2)}) copy-start(bf16[512,4096]{1,0:T(8,128)(2,1)} %ow.1) | copy-start | bytes 12582916
  49.9 7.3 %copy-start.4 = (f32[1024,512]{1,0:T(8,128)S(1)}, f32[1024,512]{1,0:T(8,128)}, u32[]{:S(2)}) copy-start(f32[1024,512]{1,0:T(8,128)} %constant.21.clone) | copy-start | bytes 6291460
  51.8 7.2 %copy-start.21 = (f32[128]{0:T(128)}, f32[128]{0:T(128)S(1)}, u32[]{:S(2)}) copy-start(f32[128]{0:T(128)S(1)} %get-tuple-element.17) | copy-start | bytes 1540
  51.8 7.2 %copy-start.23 = (f32[128]{0:T(128)}, f32[128]{0:T(128)S(1)}, u32[]{:S(2)}) copy-start(f32[128]{0:T(128)S(1)} %get-tuple-element.18) | copy-start | bytes 1540
  51.8 7.2 %copy-start.25 = (f32[128]{0:T(128)}, f32[128]{0:T(128)S(1)}, u32[]{:S(2)}) copy-start(f32[128]{0:T(128)S(1)} %get-tuple-element.19) | copy-start | bytes 1540
  51.8 16.8 %copy-start.27 = (f32[128]{0:T(128)}, f32[128]{0:T(128)S(1)}, u32[]{:S(2)}) copy-start(f32[128]{0:T(128)S(1)} %get-tuple-element.14) | copy-start | bytes 1540
  51.9 16.8 %copy-start.28 = (f32[128]{0:T(128)}, f32[128]{0:T(128)S(1)}, u32[]{:S(2)}) copy-start(f32[128]{0:T(128)S(1)} %get-tuple-element.20) | copy-start | bytes 1540
  51.9 16.8 %copy-start.29 = (f32[128]{0:T(128)}, f32[128]{0:T(128)S(1)}, u32[]{:S(2)}) copy-start(f32[128]{0:T(128)S(1)} %get-tuple-element.21) | copy-start | bytes 1540
  53.6 5.5 %copy-start.16 = (f32[512,128]{0,1:T(8,128)}, f32[512,128]{0,1:T(8,128)S(1)}, u32[]{:S(2)}) copy-start(f32[512,128]{0,1:T(8,128)S(1)} %get-tuple-element.28) | copy-start | bytes 786436
  53.6 12.8 %copy-start.30 = (f32[128]{0:T(128)}, f32[128]{0:T(128)S(1)}, u32[]{:S(2)}) copy-start(f32[128]{0:T(128)S(1)} %get-tuple-element.24) | copy-start | bytes 1540
  53.6 15.0 %copy-start.32 = (f32[128]{0:T(128)}, f32[128]{0:T(128)S(1)}, u32[]{:S(2)}) copy-start(f32[128]{0:T(128)S(1)} %get-tuple-element.23) | copy-start | bytes 1540
  61.8 4.0 %copy-start.5 = (f32[512,512]{1,0:T(8,128)S(1)}, f32[512,512]{1,0:T(8,128)}, u32[]{:S(2)}) copy-start(f32[512,512]{1,0:T(8,128)} %constant.46) | copy-start | bytes 3145732
  63.7 2.1 %copy-start.19 = (f32[1024,128]{1,0:T(8,128)S(1)}, f32[1024,128]{1,0:T(8,128)}, u32[]{:S(2)}) copy-start(f32[1024,128]{1,0:T(8,128)} %fusion.127) | copy-start | bytes 1572868
  63.7 2.6 %copy-start.6 = (f32[512,512]{1,0:T(8,128)S(1)}, f32[512,512]{1,0:T(8,128)}, u32[]{:S(2)}) copy-start(f32[512,512]{1,0:T(8,128)} %constant.47) | copy-start | bytes 3145732
  63.7 2.7 %copy-start.17 = (f32[512,128]{0,1:T(8,128)S(1)}, f32[512,128]{0,1:T(8,128)}, u32[]{:S(2)}) copy-start(f32[512,128]{0,1:T(8,128)} %copy-done.16) | copy-start | bytes 786436
  65.9 1.1 copy-start.8
  67.0 1.7 %copy-start.12 = (f32[512,128]{0,1:T(8,128)}, f32[512,128]{0,1:T(8,128)S(1)}, u32[]{:S(2)}) copy-start(f32[512,128]{0,1:T(8,128)S(1)} %fusion.13) | copy-start | bytes 786436
  67.0 1.1 copy-start.10
  67.0 1.7 %copy-start.14 = (f32[512,128]{0,1:T(8,128)S(1)}, f32[512,128]{0,1:T(8,128)}, u32[]{:S(2)}) copy-start(f32[512,128]{0,1:T(8,128)} %copy.84) | copy-start | bytes 786436
  67.0 1.7 %copy-start.20 = (f32[512,128]{0,1:T(8,128)S(1)}, f32[512,128]{0,1:T(8,128)}, u32[]{:S(2)}) copy-start(f32[512,128]{0,1:T(8,128)} %copy.69) | copy-start | bytes 786436
  70.8 12.1 %all-to-all-start.1 = ((bf16[4,128,128]{1,2,0:T(8,128)(2,1)}), bf16[4,128,128]{1,2,0:T(8,128)(2,1)S(1)}, u32[]{:S(2)}, u32[]{:S(2)}) async-start(bf16[4,128,128]{1,2,0:T(8,128)(2,1)} %bitcast.114), calls=%async_computation.1 | async-start | bytes 262144 | tf_op jit(solution)/shard_map/all_to_all | solution.py:92
  74.3 3.7 %copy-start.11 = (f32[1024,128]{1,0:T(8,128)S(1)}, f32[1024,128]{1,0:T(8,128)}, u32[]{:S(2)}) copy-start(f32[1024,128]{1,0:T(8,128)} %fusion.129) | copy-start | bytes 1572868
  75.8 2.8 %copy-start.7 = (f32[512,512]{1,0:T(8,128)S(1)}, f32[512,512]{1,0:T(8,128)}, u32[]{:S(2)}) copy-start(f32[512,512]{1,0:T(8,128)} %constant.47) | copy-start | bytes 3145732
  75.8 2.8 %copy-start.13 = (f32[512,128]{0,1:T(8,128)S(1)}, f32[512,128]{0,1:T(8,128)}, u32[]{:S(2)}) copy-start(f32[512,128]{0,1:T(8,128)} %copy-done.12) | copy-start | bytes 786436
  75.8 2.8 %copy-start.15 = (f32[512,128]{0,1:T(8,128)S(1)}, f32[512,128]{0,1:T(8,128)}, u32[]{:S(2)}) copy-start(f32[512,128]{0,1:T(8,128)} %copy.84) | copy-start | bytes 786436
  75.8 2.8 %copy-start.18 = (f32[512,128]{0,1:T(8,128)S(1)}, f32[512,128]{0,1:T(8,128)}, u32[]{:S(2)}) copy-start(f32[512,128]{0,1:T(8,128)} %get-tuple-element.3) | copy-start | bytes 786436
  75.8 2.8 %copy-start.33 = (f32[128]{0:T(128)S(1)}, f32[128]{0:T(128)}, u32[]{:S(2)}) copy-start(f32[128]{0:T(128)} %copy-done.32) | copy-start | bytes 1540
  78.0 1.2 copy-start.22
  78.0 1.2 copy-start.24
  78.0 1.2 copy-start.26
  79.1 1.3 copy-start.9
  79.4 1.6 copy-start.31
  82.9 12.3 %all-to-all-start.3 = ((bf16[3,512,128]{2,0,1:T(4,128)(2,1)}), bf16[3,512,128]{2,0,1:T(4,128)(2,1)S(1)}, u32[]{:S(2)}, u32[]{:S(2)}) async-start(bf16[3,512,128]{2,0,1:T(4,128)(2,1)} %copy.86), calls=%async_computation.3 | async-start | bytes 1048576 | tf_op jit(solution)/shard_map/all_to_all | solution.py:92
  95.2 33.0 %all-to-all-start.2 = ((bf16[8,128,512]{2,1,0:T(8,128)(2,1)}), bf16[8,128,512]{2,1,0:T(8,128)(2,1)S(1)}, u32[]{:S(2)}, u32[]{:S(2)}) async-start(bf16[8,128,512]{2,1,0:T(8,128)(2,1)} %bitcast.113), calls=%async_computation.2 | async-start | bytes 2097152 | tf_op jit(solution)/shard_map/all_to_all | solution.py:99
  128.2 29.4 %all-to-all-start.4 = ((bf16[8,128,512]{2,1,0:T(8,128)(2,1)}), bf16[8,128,512]{2,1,0:T(8,128)(2,1)S(1)}, u32[]{:S(2)}, u32[]{:S(2)}) async-start(bf16[8,128,512]{2,1,0:T(8,128)(2,1)} %bitcast.111), calls=%async_computation.4 | async-start | bytes 2097152 | tf_op jit(solution)/shard_map/all_to_all | solution.py:99

commit v3 on v2

--- a/solution.py
+++ b/solution.py
@@ -112,7 +112,7 @@
 
 
 def project_kernel(
-    chan_count, seq_count, tok, cot, w, ow, out,
+    chan_count, seq_count, tok, cot, w, ow, filters, out, filt,
     tok_all, cot_all, w_all, ow_all, acc, grad,
     w_sem, send_sem, recv_sem, seq_send, seq_recv, own_sem,
 ):
@@ -148,6 +148,28 @@
         )
 
     held = [{}, {}]
+
+    def spread(source, target, where):
+        copies = []
+        for k in range(1, seq_count):
+            peer = seq_peer(k)
+            lanes = pl.ds(pl.multiple_of(peer * part, part), part)
+            copies.append(
+                pltpu.make_async_remote_copy(
+                    src_ref=source.at[:, :, lanes],
+                    dst_ref=target,
+                    send_sem=seq_send.at[where, k],
+                    recv_sem=seq_recv.at[where, k],
+                    device_id={"seq": peer},
+                    device_id_type=MESH,
+                )
+            )
+        lanes = pl.ds(pl.multiple_of(row * part, part), part)
+        own = pltpu.make_async_copy(source.at[:, :, lanes], target, own_sem.at[where])
+        for copy in copies + [own]:
+            copy.start()
+        return copies + [own]
+
     for which, source in enumerate((tok, cot)):
         for k in range(1, outer_count):
             held[which][k] = push(which, source, column(k, inner), me, k)
@@ -176,6 +198,7 @@
         )
         grad[0] = product if first else grad[0] + product
 
+    last = spread(filters, filt.at[:, row], 2)
     for load in loads[:3]:
         load.wait()
     add_tok(tok[...], me, True)
@@ -193,35 +216,14 @@
         owner = column(-k, 1 - inner)
         add_tok(tok_all[owner], owner)
 
-    def spread(source, slots, where):
-        copies = []
-        for k in range(1, seq_count):
-            peer = seq_peer(k)
-            lanes = pl.ds(pl.multiple_of(peer * part, part), part)
-            copies.append(
-                pltpu.make_async_remote_copy(
-                    src_ref=source.at[:, :, lanes],
-                    dst_ref=out.at[slots, row],
-                    send_sem=seq_send.at[where, k],
-                    recv_sem=seq_recv.at[where, k],
-                    device_id={"seq": peer},
-                    device_id_type=MESH,
-                )
-            )
-        lanes = pl.ds(pl.multiple_of(row * part, part), part)
-        own = pltpu.make_async_copy(source.at[:, :, lanes], out.at[slots, row], own_sem.at[where])
-        for copy in copies + [own]:
-            copy.start()
-        return copies + [own]
-
-    last = spread(acc, pl.ds(0, 3), 0)
+    last = last + spread(acc, out.at[pl.ds(0, 3), row], 0)
     held[1][0].wait_recv()
     add_cot(cot_all[partner], partner)
     for k in range(1, outer_count):
         held[1][outer_count - 1 + k].wait_recv()
         owner = column(-k, 1 - inner)
         add_cot(cot_all[owner], owner)
-    last = last + spread(grad, pl.ds(3, 1), 1)
+    last = last + spread(grad, out.at[pl.ds(3, 1), row], 1)
     for copies in held:
         for copy in copies.values():
             copy.wait_send()
@@ -229,7 +231,7 @@
         copy.wait()
 
 
-def project(tokens, cotangent, weights, out_weight):
+def project(tokens, cotangent, weights, out_weight, filters):
     chan_count, seq_count = lax.axis_size("chan"), lax.axis_size("seq")
     rows, depth = tokens.shape
     chans = weights.shape[2]
@@ -237,9 +239,12 @@
     anywhere = pl.BlockSpec(memory_space=pl.ANY)
     return pl.pallas_call(
         functools.partial(project_kernel, chan_count, seq_count),
-        out_shape=jax.ShapeDtypeStruct((4, seq_count, rows, chans // seq_count), jnp.float32),
-        in_specs=[vmem, vmem, anywhere, anywhere],
-        out_specs=vmem,
+        out_shape=[
+            jax.ShapeDtypeStruct((count, seq_count, rows, chans // seq_count), jnp.float32)
+            for count in (4, 2)
+        ],
+        in_specs=[vmem, vmem, anywhere, anywhere, vmem],
+        out_specs=[vmem, vmem],
         scratch_shapes=[
             pltpu.VMEM((chan_count, rows, depth), jnp.bfloat16),
             pltpu.VMEM((chan_count, rows, depth), jnp.bfloat16),
@@ -250,14 +255,248 @@
             pltpu.SemaphoreType.DMA((4,)),
             pltpu.SemaphoreType.DMA((2, chan_count)),
             pltpu.SemaphoreType.DMA((2, chan_count)),
-            pltpu.SemaphoreType.DMA((2, seq_count)),
-            pltpu.SemaphoreType.DMA((2, seq_count)),
-            pltpu.SemaphoreType.DMA((2,)),
+            pltpu.SemaphoreType.DMA((3, seq_count)),
+            pltpu.SemaphoreType.DMA((3, seq_count)),
+            pltpu.SemaphoreType.DMA((3,)),
         ],
         compiler_params=pltpu.CompilerParams(
             collective_id=0, has_side_effects=True, vmem_limit_bytes=40 * 2**20
         ),
-    )(tokens, cotangent, weights, out_weight)
+    )(tokens, cotangent, weights, out_weight, filters)
+
+
+def split(value):
+    high = value.astype(jnp.bfloat16)
+    return high, (value - high.astype(jnp.float32)).astype(jnp.bfloat16)
+
+
+def table_dot(high, low, value):
+    top, rest = split(value)
+    wide = jnp.dot(high, jnp.concatenate([top, rest], axis=1), preferred_element_type=jnp.float32)
+    lanes = value.shape[1]
+    small = jnp.dot(low, top, preferred_element_type=jnp.float32)
+    return wide[:, :lanes] + (wide[:, lanes:] + small)
+
+
+def middle_kernel(
+    both, filters, taps, skip, high, low, back_high, back_low, second, grads, spec_one, spec_two
+):
+    length = filters.shape[1]
+    count = taps.shape[0]
+    rows = lax.broadcasted_iota(jnp.int32, filters.shape[1:], 0)
+
+    def ahead(signal):
+        return table_dot(high[...], low[...], signal)
+
+    def conv(signal, spec, conjugate):
+        product = times(ahead(signal), spec[...], conjugate)
+        return table_dot(back_high[...], back_low[...], product) * (1.0 / length)
+
+    def shifted(value, by):
+        if by > 0:
+            return jnp.where(rows < by, 0.0, pltpu.roll(value, by, 0))
+        return jnp.where(rows >= length + by, 0.0, pltpu.roll(value, length + by, 0))
+
+    def short(value, j, sign):
+        total = taps[0, j : j + 1] * value
+        for a in range(1, count):
+            total = total + taps[a, j : j + 1] * shifted(value, sign * a)
+        return total
+
+    spec_one[...] = ahead(filters[0])
+    spec_two[...] = ahead(filters[1])
+    values, gate_one, gate_two = [short(both[j], j, 1) for j in range(3)]
+    conv_one = conv(values, spec_one, False) + skip[0:1] * values
+    first_out = gate_one * conv_one
+    conv_two = conv(first_out, spec_two, False) + skip[1:2] * first_out
+    second[...] = (gate_two * conv_two).astype(jnp.bfloat16)
+    grads[2] = short(both[3] * conv_two, 2, -1).astype(jnp.bfloat16)
+    grad_conv_two = both[3] * gate_two
+    grad_first = conv(grad_conv_two, spec_two, True) + skip[1:2] * grad_conv_two
+    grads[1] = short(grad_first * conv_one, 1, -1).astype(jnp.bfloat16)
+    grad_conv_one = grad_first * gate_one
+    grad_values = conv(grad_conv_one, spec_one, True) + skip[0:1] * grad_conv_one
+    grads[0] = short(grad_values, 0, -1).astype(jnp.bfloat16)
+
+
+def fused_middle(both, filters, taps, skip, table):
+    length, lanes = filters.shape[1:]
+
+    def halves(array):
+        high = array.astype(jnp.bfloat16)
+        return high, (array - high.astype(np.float32)).astype(jnp.bfloat16)
+
+    tables = halves(table) + halves(np.ascontiguousarray(table.T))
+    return pl.pallas_call(
+        middle_kernel,
+        out_shape=[
+            jax.ShapeDtypeStruct((length, lanes), jnp.bfloat16),
+            jax.ShapeDtypeStruct((3, length, lanes), jnp.bfloat16),
+        ],
+        in_specs=[pl.BlockSpec(memory_space=pltpu.VMEM)] * 8,
+        out_specs=[pl.BlockSpec(memory_space=pltpu.VMEM)] * 2,
+        scratch_shapes=[pltpu.VMEM((2 * length, lanes), jnp.float32)] * 2,
+        compiler_params=pltpu.CompilerParams(vmem_limit_bytes=40 * 2**20),
+    )(both, filters, taps, skip, *[jnp.asarray(t) for t in tables])
+
+
+def output_kernel(
+    chan_count, seq_count, sec, grads, w, ow, mixed, token_grad,
+    sec_all, grads_all, w_all, ow_all, mine, sent, came, sum_sent, sum_came,
+    w_sem, seq_send, seq_recv, pair_send, pair_recv, sum_send, sum_recv, own_sem,
+):
+    me, row = lax.axis_index("chan"), lax.axis_index("seq")
+    outer_count = chan_count // 2
+    outer, inner = me // 2, lax.rem(me, 2)
+    partner = outer * 2 + 1 - inner
+    depth = mixed.shape[1]
+    part = sec.shape[2]
+    loads = [pltpu.make_async_copy(ow, ow_all, w_sem.at[3])]
+    loads = loads + [pltpu.make_async_copy(w.at[j], w_all.at[j], w_sem.at[j]) for j in range(3)]
+    for load in loads:
+        load.start()
+
+    def column(k, side):
+        return lax.rem(outer + k, outer_count) * 2 + side
+
+    def seq_peer(k):
+        return lax.rem(row + k, seq_count)
+
+    chan_peers = [partner] + [column(k, inner) for k in range(1, outer_count)]
+    greet(chan_peers, [seq_peer(k) for k in range(1, seq_count)])
+    lanes = pl.ds(pl.multiple_of(row * part, part), part)
+    targets = (sec_all.at[:, lanes], grads_all.at[:, :, lanes])
+
+    def source(which, peer):
+        return sec.at[peer] if which == 0 else grads.at[:, peer]
+
+    moves = [[], []]
+    for which in range(2):
+        for k in range(1, seq_count):
+            moves[which].append(
+                pltpu.make_async_remote_copy(
+                    src_ref=source(which, seq_peer(k)),
+                    dst_ref=targets[which],
+                    send_sem=seq_send.at[which, k],
+                    recv_sem=seq_recv.at[which, k],
+                    device_id={"seq": seq_peer(k)},
+                    device_id_type=MESH,
+                )
+            )
+        moves[which].append(
+            pltpu.make_async_copy(source(which, row), targets[which], own_sem.at[which])
+        )
+        for move in moves[which]:
+            move.start()
+
+    def partial(which, owner):
+        lines = pl.ds(pl.multiple_of(owner * depth, depth), depth)
+        if which == 0:
+            return jnp.dot(sec_all[...], ow_all[:, lines], preferred_element_type=jnp.float32)
+        total = 0.0
+        for j in range(3):
+            total = total + lax.dot_general(
+                grads_all[j],
+                w_all[j, lines, :],
+                (((1,), (1,)), ((), ())),
+                preferred_element_type=jnp.float32,
+            )
+        return total
+
+    pairs, sums = [{}, {}], [{}, {}]
+    order = list(range(1, outer_count)) + [0]
+
+    def make(which, k):
+        sent[which, k] = partial(which, column(k, 1 - inner)).astype(jnp.bfloat16)
+        pairs[which][k] = pltpu.make_async_remote_copy(
+            src_ref=sent.at[which, k],
+            dst_ref=came.at[which, k],
+            send_sem=pair_send.at[which, k],
+            recv_sem=pair_recv.at[which, k],
+            device_id={"chan": partner},
+            device_id_type=MESH,
+        )
+        pairs[which][k].start()
+        mine[which, k] = partial(which, column(k, inner))
+
+    def reduce_pair(which, k):
+        pairs[which][k].wait_recv()
+        total = mine[which, k] + came[which, k].astype(jnp.float32)
+        if k == 0:
+            mine[which, 0] = total
+            return
+        sum_sent[which, k] = total.astype(jnp.bfloat16)
+        sums[which][k] = pltpu.make_async_remote_copy(
+            src_ref=sum_sent.at[which, k],
+            dst_ref=sum_came.at[which, k],
+            send_sem=sum_send.at[which, k],
+            recv_sem=sum_recv.at[which, k],
+            device_id={"chan": column(k, inner)},
+            device_id_type=MESH,
+        )
+        sums[which][k].start()
+
+    def finish(which, out):
+        total = mine[which, 0]
+        for k in range(1, outer_count):
+            sums[which][k].wait_recv()
+            total = total + sum_came[which, k].astype(jnp.float32)
+        out[...] = total.astype(jnp.bfloat16)
+
+    for move in moves[0]:
+        move.wait()
+    loads[0].wait()
+    for k in order:
+        make(0, k)
+    for move in moves[1]:
+        move.wait()
+    for load in loads[1:]:
+        load.wait()
+    for k in order:
+        make(1, k)
+        reduce_pair(0, k)
+    for k in order:
+        reduce_pair(1, k)
+    finish(0, mixed)
+    finish(1, token_grad)
+    for which in range(2):
+        for copy in list(pairs[which].values()) + list(sums[which].values()):
+            copy.wait_send()
+
+
+def output_sums(second, grads, weights, out_weight):
+    chan_count, seq_count = lax.axis_size("chan"), lax.axis_size("seq")
+    rows = second.shape[1]
+    width, chans = weights.shape[1:]
+    depth = width // chan_count
+    outer_count = chan_count // 2
+    vmem = pl.BlockSpec(memory_space=pltpu.VMEM)
+    anywhere = pl.BlockSpec(memory_space=pl.ANY)
+    block = (2, outer_count, rows, depth)
+    return pl.pallas_call(
+        functools.partial(output_kernel, chan_count, seq_count),
+        out_shape=[jax.ShapeDtypeStruct((rows, depth), jnp.bfloat16)] * 2,
+        in_specs=[vmem, vmem, anywhere, anywhere],
+        out_specs=[vmem, vmem],
+        scratch_shapes=[
+            pltpu.VMEM((rows, chans), jnp.bfloat16),
+            pltpu.VMEM((3, rows, chans), jnp.bfloat16),
+            pltpu.VMEM(weights.shape, jnp.bfloat16),
+            pltpu.VMEM(out_weight.shape, jnp.bfloat16),
+            pltpu.VMEM(block, jnp.float32),
+        ]
+        + [pltpu.VMEM(block, jnp.bfloat16)] * 4
+        + [
+            pltpu.SemaphoreType.DMA((4,)),
+            pltpu.SemaphoreType.DMA((2, seq_count)),
+            pltpu.SemaphoreType.DMA((2, seq_count)),
+        ]
+        + [pltpu.SemaphoreType.DMA((2, outer_count))] * 4
+        + [pltpu.SemaphoreType.DMA((2,))],
+        compiler_params=pltpu.CompilerParams(
+            collective_id=1, has_side_effects=True, vmem_limit_bytes=44 * 2**20
+        ),
+    )(second, grads, weights, out_weight)
 
 
 def on_device(tokens, in_weight, short_kernel, filters, skip_gain, out_weight, cotangent):
@@ -266,26 +505,34 @@
     part = chans // seq_count
     start = lax.axis_index("seq") * part
     weights = jnp.transpose(in_weight, (1, 0, 2))
-    table = jnp.asarray(odd_table(tokens.shape[0] * seq_count))
+    rows = tokens.shape[0]
+    length = rows * seq_count
+    table = odd_table(length)
     taps = lax.dynamic_slice_in_dim(short_kernel, start, part, 2)
     skip = lax.dynamic_slice_in_dim(skip_gain, start, part, 1)
+    if part % 128 == 0 and rows % 16 == 0 and lax.axis_size("chan") % 2 == 0:
+        both, local_filters = project(tokens, cotangent, weights, out_weight, filters)
+        second_out, grads = fused_middle(
+            both.reshape(4, length, part), local_filters.reshape(2, length, part), taps, skip, table
+        )
+        return output_sums(
+            second_out.reshape(seq_count, rows, part),
+            grads.reshape(3, seq_count, rows, part),
+            weights,
+            out_weight,
+        )
     local_filters = swap_in(filters)
-    if part % 128 == 0 and tokens.shape[0] % 16 == 0 and lax.axis_size("chan") % 2 == 0:
-        both = project(tokens, cotangent, weights, out_weight)
-        both = both.reshape(4, seq_count * tokens.shape[0], part)
-        projected, grad_two = both[:3], both[3]
-    else:
-        rows = lax.all_gather(tokens, "chan", axis=1, tiled=True)
-        grad_rows = lax.all_gather(cotangent, "chan", axis=1, tiled=True)
-        projected = jnp.stack(
-            [jnp.dot(rows, weights[j], preferred_element_type=jnp.float32) for j in range(3)]
-        )
-        grad_two = lax.dot_general(
-            grad_rows, out_weight, (((1,), (1,)), ((), ())), preferred_element_type=jnp.float32
-        )
-        projected = swap_in(projected)
-        grad_two = swap_in(grad_two)
-    second_out, grads = middle(projected, grad_two, taps, local_filters, skip, table)
+    gathered = lax.all_gather(tokens, "chan", axis=1, tiled=True)
+    grad_rows = lax.all_gather(cotangent, "chan", axis=1, tiled=True)
+    projected = jnp.stack(
+        [jnp.dot(gathered, weights[j], preferred_element_type=jnp.float32) for j in range(3)]
+    )
+    grad_two = lax.dot_general(
+        grad_rows, out_weight, (((1,), (1,)), ((), ())), preferred_element_type=jnp.float32
+    )
+    second_out, grads = middle(
+        swap_in(projected), swap_in(grad_two), taps, local_filters, skip, jnp.asarray(table)
+    )
     second_out = swap_out(second_out)
     grads = swap_out(grads)
     mixed = share(jnp.dot(second_out, out_weight, preferred_element_type=jnp.float32))

time: 159 us -> 92.6 us (0.58)
  Pallas kernels: 39.8 us -> 84.5 us
  waiting for transfers between devices: 42.7 us -> 0 us
  matrix products: 29.1 us -> 0 us
  starting transfers between devices: 22.1 us -> 0 us
  local copies, waits for them, and re-layouts: 18.2 us -> 7.1 us
  other arithmetic: 5.33 us -> 0 us
    pallas_call x0 -> x2, Pallas kernels: none -> 44.8 us  [the longest x1 38.7 us: output_sums(): pl.pallas_call(functools.partial(output_kernel, chan_count, seq_count), o...]
    all_to_all x5 -> x0, waiting for transfers between devices: 42.7 us -> none  [the longest x2 37.9 us: share(): got = lax.all_to_all(sent, 'chan', 0, 0, tiled=True)]
    dot_general x18 -> x0, matrix products: 29.1 us -> none  [the longest x3 11.2 us: on_device(): lax.dot_general(grads[j], weights[j], (((1,), (1,)), ((), ())), preferred...]
    all_to_all x5 -> x0, starting transfers between devices: 22.1 us -> none  [the longest x2 10.9 us: share(): got = lax.all_to_all(sent, 'chan', 0, 0, tiled=True)]
    squeeze x4 -> x0, local copies, waits for them, and re-layouts: 4.63 us -> none  [the longest x3 2.77 us: middle(): total = taps[0, j] * projected[j]]
    slice x8 -> x0, local copies, waits for them, and re-layouts: 4.12 us -> none  [the longest x1 1.89 us: middle(): spec_one = forward(table, filters[0])]
    reshape x2 -> x0, local copies, waits for them, and re-layouts: 2.18 us -> none  [share(): partial.astype(jnp.bfloat16).reshape(rows, count, width // count)]
    another operation x4 -> x0, other arithmetic: 2 us -> none  [middle(): return (second_out, jnp.stack(grads))]
  transfers between devices with their start and end apart: 5 -> 0, of which waited for: 3 -> 0; matrix products, arithmetic and copies ran while one was open for 23% -> 0% of each run, Pallas kernels for 25% -> 0%
where the time goes in v3:
time: 92.6 us; the launch traced here: 92.3 us
  Pallas kernels  84.5 us (91%)
  local copies, waits for them, and re-layouts  7.1 us (8%)
    pallas_call x1, Pallas kernels, project(): pl.pallas_call(functools.partial(project_kernel, chan_count, seq_count),...  39.7 us
    pallas_call x1, Pallas kernels, output_sums(): pl.pallas_call(functools.partial(output_kernel, chan_count, seq_count), o...  38.7 us
    unnamed x22, local copies, waits for them, and re-layouts  6.41 us
    pallas_call x1, Pallas kernels, fused_middle(): pl.pallas_call(middle_kernel, out_shape=[jax.ShapeDtypeStruct((length, la...  6.13 us

profile of v3, /device:TPU:0, one launch (start us, length us, event | category | flops | bytes accessed | tf_op | source)
XLA Modules:
  0.0 92.3 jit_solution(509309839274551748)
XLA Ops:
  0.6 0.0 copy-start
  0.7 0.7 constant_dynamic-slice_fusion.skip
  1.3 0.0 copy-done
  1.4 0.0 copy-start.1
  1.4 2.2 %copy-done.1 = bf16[512,4096]{1,0:T(8,128)(2,1)S(1)} copy-done((bf16[512,4096]{1,0:T(8,128)(2,1)S(1)}, bf16[512,4096]{1,0:T(8,128)(2,1)}, u32[]{:S(2)}) %copy-start.1) | copy-done | bytes 4194328
  3.6 0.0 copy-start.7
  3.6 1.0 %copy-done.7 = f32[2,128,512]{2,1,0:T(8,128)S(1)} copy-done((f32[2,128,512]{2,1,0:T(8,128)S(1)}, f32[2,128,512]{2,1,0:T(8,128)}, u32[]{:S(2)}) %copy-start.7) | copy-done | bytes 524312
  4.6 0.0 copy-start.8
  4.6 0.9 copy-done.8
  5.5 0.0 copy-start.9
  5.5 0.9 copy-done.9
  6.4 0.0 copy-start.3
  6.4 0.0 copy-start.4
  6.4 0.0 copy-start.5
  6.4 0.0 copy-start.6
  6.4 0.0 copy-start.2
  6.4 39.7 %shard_map.122 = (f32[4,4,128,128]{3,2,1,0:T(8,128)S(1)}, f32[2,4,128,128]{3,2,1,0:T(8,128)S(1)}) custom-call(bf16[128,512]{1,0:T(8,128)(2,1)S(1)} %copy-done.8, bf16[128,512]{1,0:T(8,128)(2,1)S(1)} %copy-done.9, bf16[3,4096,512]{2,1,0:T(8,128)(2,1)} %bitcast.9, bf16[512,4096]{1,0:T(8,128)(2,1)S(1)} %copy-done.1, f32[2,128,512]{2,1,0:T(8,128)S(1)} %copy-done.7), custom_call_target="tpu_custom_call" | custom-call | tf_op jit(solution)/shard_map/pallas_call | solution.py:240
  46.1 0.0 copy-done.3
  46.1 0.0 copy-done.4
  46.1 0.0 copy-done.5
  46.2 0.0 copy-done.6
  46.2 6.1 %shard_map.123 = (bf16[512,128]{1,0:T(8,128)(2,1)S(1)}, bf16[3,512,128]{2,1,0:T(8,128)(2,1)S(1)}) custom-call(f32[4,512,128]{2,1,0:T(8,128)S(1)} %bitcast.5, f32[2,512,128]{2,1,0:T(8,128)S(1)} %bitcast.6, f32[3,3,128]{2,1,0:T(4,128)S(1)} %constant_dynamic-slice_fusion.1.taps, f32[2,128]{1,0:T(2,128)S(1)} %constant_dynamic-slice_fusion.skip, ...), custom_call_target="tpu_custom_call" | custom-call | tf_op jit(solution)/shard_map/pallas_call | solution.py:330
  52.3 0.0 copy-done.2
  52.3 38.7 %shard_map.124 = (bf16[128,512]{1,0:T(8,128)(2,1)S(1)}, bf16[128,512]{1,0:T(8,128)(2,1)S(1)}) custom-call(bf16[4,128,128]{2,1,0:T(8,128)(2,1)S(1)} %bitcast.8, bf16[3,4,128,128]{3,2,1,0:T(8,128)(2,1)S(1)} %bitcast.7, bf16[3,4096,512]{2,1,0:T(8,128)(2,1)} %bitcast.10, bf16[512,4096]{1,0:T(8,128)(2,1)S(1)} %copy-done.2), custom_call_target="tpu_custom_call" | custom-call | tf_op jit(solution)/shard_map/pallas_call | solution.py:476
  91.0 0.7 copy.15
  91.7 0.7 copy.16
  (1 shorter events, 0.0 us)
Async XLA Ops:
  0.6 0.7 copy-start
  1.4 2.2 %copy-start.1 = (bf16[512,4096]{1,0:T(8,128)(2,1)S(1)}, bf16[512,4096]{1,0:T(8,128)(2,1)}, u32[]{:S(2)}) copy-start(bf16[512,4096]{1,0:T(8,128)(2,1)} %ow.3) | copy-start | bytes 12582916
  3.6 1.0 %copy-start.7 = (f32[2,128,512]{2,1,0:T(8,128)S(1)}, f32[2,128,512]{2,1,0:T(8,128)}, u32[]{:S(2)}) copy-start(f32[2,128,512]{2,1,0:T(8,128)} %filters.1) | copy-start | bytes 1572868
  4.6 0.9 copy-start.8
  5.5 0.9 copy-start.9
  6.4 39.7 %copy-start.3 = (bf16[512,1024]{1,0:T(8,128)(2,1)S(1)}, bf16[512,1024]{1,0:T(8,128)(2,1)}, u32[]{:S(2)}) copy-start(bf16[512,1024]{1,0:T(8,128)(2,1)} %constant.22.clone.back_low) | copy-start | bytes 3145732
  6.4 39.7 %copy-start.4 = (bf16[512,1024]{1,0:T(8,128)(2,1)S(1)}, bf16[512,1024]{1,0:T(8,128)(2,1)}, u32[]{:S(2)}) copy-start(bf16[512,1024]{1,0:T(8,128)(2,1)} %constant.21.clone.back_high) | copy-start | bytes 3145732
  6.4 39.7 %copy-start.5 = (bf16[1024,512]{1,0:T(8,128)(2,1)S(1)}, bf16[1024,512]{1,0:T(8,128)(2,1)}, u32[]{:S(2)}) copy-start(bf16[1024,512]{1,0:T(8,128)(2,1)} %constant.20.clone.low) | copy-start | bytes 3145732
  6.4 39.7 %copy-start.6 = (bf16[1024,512]{1,0:T(8,128)(2,1)S(1)}, bf16[1024,512]{1,0:T(8,128)(2,1)}, u32[]{:S(2)}) copy-start(bf16[1024,512]{1,0:T(8,128)(2,1)} %constant.19.clone.high) | copy-start | bytes 3145732
  6.4 45.9 %copy-start.2 = (bf16[512,4096]{1,0:T(8,128)(2,1)S(1)}, bf16[512,4096]{1,0:T(8,128)(2,1)}, u32[]{:S(2)}) copy-start(bf16[512,4096]{1,0:T(8,128)(2,1)} %ow.3) | copy-start | bytes 12582916

commit v4 on v3

--- a/solution.py
+++ b/solution.py
@@ -114,7 +114,7 @@
 def project_kernel(
     chan_count, seq_count, tok, cot, w, ow, filters, out, filt,
     tok_all, cot_all, w_all, ow_all, acc, grad,
-    w_sem, send_sem, recv_sem, seq_send, seq_recv, own_sem,
+    w_sem, line_send, line_recv, pair_send, pair_recv, seq_send, seq_recv, own_sem,
 ):
     me, row = lax.axis_index("chan"), lax.axis_index("seq")
     outer_count = chan_count // 2
@@ -128,7 +128,7 @@
         load.start()
 
     def column(k, side):
-        return lax.rem(outer + k + outer_count, outer_count) * 2 + side
+        return lax.rem(outer + k, outer_count) * 2 + side
 
     def seq_peer(k):
         return lax.rem(row + k, seq_count)
@@ -136,18 +136,67 @@
     chan_peers = [partner] + [column(k, inner) for k in range(1, outer_count)]
     greet(chan_peers, [seq_peer(k) for k in range(1, seq_count)])
 
-    def push(which, source, target, owner, slot):
-        place = (tok_all, cot_all)[which].at[owner]
+    buffers = (tok_all, cot_all)
+    lines = ((0, inner), (1, inner), (1, 1 - inner))
+    ways = (1, -1)
+
+    def inside(place):
+        return jnp.logical_and(place >= 0, place < outer_count)
+
+    def owner_of(way, d, side):
+        return (outer - way * d) * 2 + side
+
+    def along(line, way, d):
+        which, side = lines[line]
+        owner = owner_of(way, d - 1, side)
+        source = (tok, cot)[which] if d == 1 and line < 2 else buffers[which].at[owner]
         return pltpu.make_async_remote_copy(
             src_ref=source,
-            dst_ref=place,
-            send_sem=send_sem.at[which, slot],
-            recv_sem=recv_sem.at[which, slot],
-            device_id={"chan": target},
+            dst_ref=buffers[which].at[owner],
+            send_sem=line_send.at[line, 1 - max(way, 0), d],
+            recv_sem=line_recv.at[line, 1 - max(way, 0), d],
+            device_id={"chan": (outer + way) * 2 + inner},
             device_id_type=MESH,
         )
 
-    held = [{}, {}]
+    def landed(line, way, d):
+        which, side = lines[line]
+        return pltpu.make_async_remote_copy(
+            src_ref=buffers[which].at[owner_of(way, d, side)],
+            dst_ref=buffers[which].at[owner_of(way, d, side)],
+            send_sem=line_send.at[line, 1 - max(way, 0), d],
+            recv_sem=line_recv.at[line, 1 - max(way, 0), d],
+            device_id={"chan": (outer - way) * 2 + inner},
+            device_id_type=MESH,
+        )
+
+    def sends(way, d):
+        return jnp.logical_and(inside(outer - way * (d - 1)), inside(outer + way))
+
+    def launch(line, d):
+        for way in ways:
+            @pl.when(sends(way, d))
+            def _():
+                along(line, way, d).start()
+
+    def across(which, owner, slot):
+        own = slot == 0
+        return pltpu.make_async_remote_copy(
+            src_ref=(tok, cot)[which] if own else buffers[which].at[owner],
+            dst_ref=buffers[which].at[owner],
+            send_sem=pair_send.at[which, slot],
+            recv_sem=pair_recv.at[which, slot],
+            device_id={"chan": partner},
+            device_id_type=MESH,
+        )
+
+    def slot_of(way, d):
+        return (1 - max(way, 0)) * (outer_count - 1) + d
+
+    firsts = [across(which, me, 0) for which in range(2)]
+    launch(0, 1)
+    for copy in firsts:
+        copy.start()
 
     def spread(source, target, where):
         copies = []
@@ -170,31 +219,16 @@
             copy.start()
         return copies + [own]
 
-    for which, source in enumerate((tok, cot)):
-        for k in range(1, outer_count):
-            held[which][k] = push(which, source, column(k, inner), me, k)
-        held[which][0] = push(which, source, partner, me, 0)
-        for copy in held[which].values():
-            copy.start()
-
-    def pass_on(which, k):
-        held[which][k].wait_recv()
-        owner = column(-k, inner)
-        slot = outer_count - 1 + k
-        held[which][slot] = push(which, (tok_all, cot_all)[which].at[owner], partner, owner, slot)
-        held[which][slot].start()
-        return owner
-
     def add_tok(block, owner, first=False):
-        lines = pl.ds(pl.multiple_of(owner * depth, depth), depth)
+        span = pl.ds(pl.multiple_of(owner * depth, depth), depth)
         for j in range(3):
-            product = jnp.dot(block, w_all[j, lines, :], preferred_element_type=jnp.float32)
+            product = jnp.dot(block, w_all[j, span, :], preferred_element_type=jnp.float32)
             acc[j] = product if first else acc[j] + product
 
     def add_cot(block, owner, first=False):
-        lines = pl.ds(pl.multiple_of(owner * depth, depth), depth)
+        span = pl.ds(pl.multiple_of(owner * depth, depth), depth)
         product = lax.dot_general(
-            block, ow_all[:, lines], (((1,), (1,)), ((), ())), preferred_element_type=jnp.float32
+            block, ow_all[:, span], (((1,), (1,)), ((), ())), preferred_element_type=jnp.float32
         )
         grad[0] = product if first else grad[0] + product
 
@@ -202,31 +236,61 @@
     for load in loads[:3]:
         load.wait()
     add_tok(tok[...], me, True)
-    for k in range(1, outer_count):
-        owner = pass_on(0, k)
-        add_tok(tok_all[owner], owner)
-    held[0][0].wait_recv()
+
+    def step(line, d):
+        which, side = lines[line]
+        for way in ways:
+            @pl.when(inside(outer - way * d))
+            def _():
+                landed(line, way, d).wait_recv()
+                if d + 1 < outer_count:
+                    @pl.when(inside(outer + way))
+                    def _():
+                        along(line, way, d + 1).start()
+                owner = owner_of(way, d, side)
+                if line == 0:
+                    across(0, owner, slot_of(way, d)).start()
+                    add_tok(tok_all[owner], owner)
+                else:
+                    add_cot(cot_all[owner], owner)
+
+    loads[3].wait()
+    launch(1, 1)
+    step(0, 1)
+    firsts[1].wait_recv()
+    launch(2, 1)
+    add_cot(cot[...], me, True)
+    add_cot(cot_all[partner], partner)
+    firsts[0].wait_recv()
     add_tok(tok_all[partner], partner)
-    loads[3].wait()
-    add_cot(cot[...], me, True)
-    for k in range(1, outer_count):
-        owner = pass_on(1, k)
-        add_cot(cot_all[owner], owner)
-        held[0][outer_count - 1 + k].wait_recv()
-        owner = column(-k, 1 - inner)
-        add_tok(tok_all[owner], owner)
+    for d in range(1, outer_count):
+        if d > 1:
+            step(0, d)
+        step(1, d)
+        step(2, d)
+    for d in range(1, outer_count):
+        for way in ways:
+            @pl.when(inside(outer - way * d))
+            def _():
+                owner = owner_of(way, d, 1 - inner)
+                across(0, owner, slot_of(way, d)).wait_recv()
+                add_tok(tok_all[owner], owner)
 
     last = last + spread(acc, out.at[pl.ds(0, 3), row], 0)
-    held[1][0].wait_recv()
-    add_cot(cot_all[partner], partner)
-    for k in range(1, outer_count):
-        held[1][outer_count - 1 + k].wait_recv()
-        owner = column(-k, 1 - inner)
-        add_cot(cot_all[owner], owner)
     last = last + spread(grad, out.at[pl.ds(3, 1), row], 1)
-    for copies in held:
-        for copy in copies.values():
-            copy.wait_send()
+    for copy in firsts:
+        copy.wait_send()
+    for d in range(1, outer_count):
+        for way in ways:
+            @pl.when(sends(way, d))
+            def _():
+                for line in range(3):
+                    along(line, way, d).wait_send()
+
+            @pl.when(inside(outer - way * d))
+            def _():
+                across(0, owner_of(way, d, inner), slot_of(way, d)).wait_send()
+
     for copy in last:
         copy.wait()
 
@@ -243,7 +307,7 @@
             jax.ShapeDtypeStruct((count, seq_count, rows, chans // seq_count), jnp.float32)
             for count in (4, 2)
         ],
-        in_specs=[vmem, vmem, anywhere, anywhere, vmem],
+        in_specs=[vmem, vmem, anywhere, anywhere, anywhere],
         out_specs=[vmem, vmem],
         scratch_shapes=[
             pltpu.VMEM((chan_count, rows, depth), jnp.bfloat16),
@@ -253,12 +317,19 @@
             pltpu.VMEM((3, rows, chans), jnp.float32),
             pltpu.VMEM((1, rows, chans), jnp.float32),
             pltpu.SemaphoreType.DMA((4,)),
+            pltpu.SemaphoreType.DMA((3, 2, chan_count // 2)),
+            pltpu.SemaphoreType.DMA((3, 2, chan_count // 2)),
             pltpu.SemaphoreType.DMA((2, chan_count)),
             pltpu.SemaphoreType.DMA((2, chan_count)),
             pltpu.SemaphoreType.DMA((3, seq_count)),
             pltpu.SemaphoreType.DMA((3, seq_count)),
             pltpu.SemaphoreType.DMA((3,)),
         ],
+        cost_estimate=pl.CostEstimate(
+            flops=2 * rows * depth * chan_count * chans * 4,
+            bytes_accessed=2 * depth * chan_count * chans * 4,
+            transcendentals=0,
+        ),
         compiler_params=pltpu.CompilerParams(
             collective_id=0, has_side_effects=True, vmem_limit_bytes=40 * 2**20
         ),

time: 92.6 us -> 96.6 us (1.043)
  Pallas kernels: 84.5 us -> 88.4 us
    pallas_call x1, Pallas kernels: 39.7 us -> 46 us  [project(): pl.pallas_call(functools.partial(project_kernel, chan_count, seq_count),...]
    pallas_call x1, Pallas kernels: 38.7 us -> 36.3 us  [output_sums(): pl.pallas_call(functools.partial(output_kernel, chan_count, seq_count), o...]
where the time goes in v4:
time: 96.6 us; the launch traced here: 96.3 us
  Pallas kernels  88.4 us (92%)
  local copies, waits for them, and re-layouts  7.1 us (7%)
    pallas_call x1, Pallas kernels, project(): pl.pallas_call(functools.partial(project_kernel, chan_count, seq_count),...  46 us
    pallas_call x1, Pallas kernels, output_sums(): pl.pallas_call(functools.partial(output_kernel, chan_count, seq_count), o...  36.3 us
    unnamed x22, local copies, waits for them, and re-layouts  6.41 us
    pallas_call x1, Pallas kernels, fused_middle(): pl.pallas_call(middle_kernel, out_shape=[jax.ShapeDtypeStruct((length, la...  6.12 us

profile of v4, /device:TPU:0, one launch (start us, length us, event | category | flops | bytes accessed | tf_op | source)
XLA Modules:
  0.0 96.3 jit_solution(7589788121272730982)
XLA Ops:
  0.6 0.0 copy-start
  0.7 0.7 constant_dynamic-slice_fusion.skip
  1.3 0.0 copy-done
  1.4 0.0 copy-start.1
  1.4 2.2 %copy-done.1 = bf16[512,4096]{1,0:T(8,128)(2,1)S(1)} copy-done((bf16[512,4096]{1,0:T(8,128)(2,1)S(1)}, bf16[512,4096]{1,0:T(8,128)(2,1)}, u32[]{:S(2)}) %copy-start.1) | copy-done | bytes 4194328
  3.6 0.0 copy-start.7
  3.6 1.0 %copy-done.7 = f32[2,128,512]{2,1,0:T(8,128)S(1)} copy-done((f32[2,128,512]{2,1,0:T(8,128)S(1)}, f32[2,128,512]{2,1,0:T(8,128)}, u32[]{:S(2)}) %copy-start.7) | copy-done | bytes 524312
  4.6 0.0 copy-start.8
  4.6 0.9 copy-done.8
  5.5 0.0 copy-start.9
  5.5 0.9 copy-done.9
  6.4 0.0 copy-start.3
  6.4 0.0 copy-start.4
  6.4 0.0 copy-start.5
  6.4 0.0 copy-start.6
  6.4 0.0 copy-start.2
  6.4 46.0 %shard_map.122 = (f32[4,4,128,128]{3,2,1,0:T(8,128)S(1)}, f32[2,4,128,128]{3,2,1,0:T(8,128)S(1)}) custom-call(bf16[128,512]{1,0:T(8,128)(2,1)S(1)} %copy-done.8, bf16[128,512]{1,0:T(8,128)(2,1)S(1)} %copy-done.9, bf16[3,4096,512]{2,1,0:T(8,128)(2,1)} %bitcast.9, bf16[512,4096]{1,0:T(8,128)(2,1)S(1)} %copy-done.1, f32[2,128,512]{2,1,0:T(8,128)S(1)} %copy-done.7), custom_call_target="tpu_custom_call" | custom-call | flops 2147483648 | bytes 16777216 | tf_op jit(solution)/shard_map/pallas_call | solution.py:304
  52.4 0.0 copy-done.3
  52.5 0.0 copy-done.4
  52.5 0.0 copy-done.5
  52.5 0.0 copy-done.6
  52.5 6.1 %shard_map.123 = (bf16[512,128]{1,0:T(8,128)(2,1)S(1)}, bf16[3,512,128]{2,1,0:T(8,128)(2,1)S(1)}) custom-call(f32[4,512,128]{2,1,0:T(8,128)S(1)} %bitcast.5, f32[2,512,128]{2,1,0:T(8,128)S(1)} %bitcast.6, f32[3,3,128]{2,1,0:T(4,128)S(1)} %constant_dynamic-slice_fusion.1.taps, f32[2,128]{1,0:T(2,128)S(1)} %constant_dynamic-slice_fusion.skip, ...), custom_call_target="tpu_custom_call" | custom-call | tf_op jit(solution)/shard_map/pallas_call | solution.py:401
  58.6 0.0 copy-done.2
  58.6 36.3 %shard_map.124 = (bf16[128,512]{1,0:T(8,128)(2,1)S(1)}, bf16[128,512]{1,0:T(8,128)(2,1)S(1)}) custom-call(bf16[4,128,128]{2,1,0:T(8,128)(2,1)S(1)} %bitcast.8, bf16[3,4,128,128]{3,2,1,0:T(8,128)(2,1)S(1)} %bitcast.7, bf16[3,4096,512]{2,1,0:T(8,128)(2,1)} %bitcast.10, bf16[512,4096]{1,0:T(8,128)(2,1)S(1)} %copy-done.2), custom_call_target="tpu_custom_call" | custom-call | tf_op jit(solution)/shard_map/pallas_call | solution.py:547
  95.0 0.7 copy.15
  95.6 0.7 copy.16
  (1 shorter events, 0.0 us)
Async XLA Ops:
  0.6 0.7 copy-start
  1.4 2.2 %copy-start.1 = (bf16[512,4096]{1,0:T(8,128)(2,1)S(1)}, bf16[512,4096]{1,0:T(8,128)(2,1)}, u32[]{:S(2)}) copy-start(bf16[512,4096]{1,0:T(8,128)(2,1)} %ow.3) | copy-start | bytes 12582916
  3.6 1.0 %copy-start.7 = (f32[2,128,512]{2,1,0:T(8,128)S(1)}, f32[2,128,512]{2,1,0:T(8,128)}, u32[]{:S(2)}) copy-start(f32[2,128,512]{2,1,0:T(8,128)} %filters.1) | copy-start | bytes 1572868
  4.6 0.9 copy-start.8
  5.5 0.9 copy-start.9
  6.4 46.0 %copy-start.3 = (bf16[512,1024]{1,0:T(8,128)(2,1)S(1)}, bf16[512,1024]{1,0:T(8,128)(2,1)}, u32[]{:S(2)}) copy-start(bf16[512,1024]{1,0:T(8,128)(2,1)} %constant.22.clone.back_low) | copy-start | bytes 3145732
  6.4 46.0 %copy-start.4 = (bf16[512,1024]{1,0:T(8,128)(2,1)S(1)}, bf16[512,1024]{1,0:T(8,128)(2,1)}, u32[]{:S(2)}) copy-start(bf16[512,1024]{1,0:T(8,128)(2,1)} %constant.21.clone.back_high) | copy-start | bytes 3145732
  6.4 46.0 %copy-start.5 = (bf16[1024,512]{1,0:T(8,128)(2,1)S(1)}, bf16[1024,512]{1,0:T(8,128)(2,1)}, u32[]{:S(2)}) copy-start(bf16[1024,512]{1,0:T(8,128)(2,1)} %constant.20.clone.low) | copy-start | bytes 3145732
  6.4 46.1 %copy-start.6 = (bf16[1024,512]{1,0:T(8,128)(2,1)S(1)}, bf16[1024,512]{1,0:T(8,128)(2,1)}, u32[]{:S(2)}) copy-start(bf16[1024,512]{1,0:T(8,128)(2,1)} %constant.19.clone.high) | copy-start | bytes 3145732
  6.4 52.2 %copy-start.2 = (bf16[512,4096]{1,0:T(8,128)(2,1)S(1)}, bf16[512,4096]{1,0:T(8,128)(2,1)}, u32[]{:S(2)}) copy-start(bf16[512,4096]{1,0:T(8,128)(2,1)} %ow.3) | copy-start | bytes 12582916

commit v5 on v3

--- a/solution.py
+++ b/solution.py
@@ -124,7 +124,9 @@
     part = out.shape[3]
     loads = [pltpu.make_async_copy(w.at[j], w_all.at[j], w_sem.at[j]) for j in range(3)]
     loads.append(pltpu.make_async_copy(ow, ow_all, w_sem.at[3]))
-    for load in loads:
+    loads.append(pltpu.make_async_copy(tok, tok_all.at[me], w_sem.at[4]))
+    loads.append(pltpu.make_async_copy(cot, cot_all.at[me], w_sem.at[5]))
+    for load in loads[4:] + loads[:4]:
         load.start()
 
     def column(k, side):
@@ -199,16 +201,17 @@
         grad[0] = product if first else grad[0] + product
 
     last = spread(filters, filt.at[:, row], 2)
-    for load in loads[:3]:
+    for load in loads[:3] + [loads[4]]:
         load.wait()
-    add_tok(tok[...], me, True)
+    add_tok(tok_all[me], me, True)
     for k in range(1, outer_count):
         owner = pass_on(0, k)
         add_tok(tok_all[owner], owner)
     held[0][0].wait_recv()
     add_tok(tok_all[partner], partner)
     loads[3].wait()
-    add_cot(cot[...], me, True)
+    loads[5].wait()
+    add_cot(cot_all[me], me, True)
     for k in range(1, outer_count):
         owner = pass_on(1, k)
         add_cot(cot_all[owner], owner)
@@ -243,7 +246,7 @@
             jax.ShapeDtypeStruct((count, seq_count, rows, chans // seq_count), jnp.float32)
             for count in (4, 2)
         ],
-        in_specs=[vmem, vmem, anywhere, anywhere, vmem],
+        in_specs=[anywhere] * 5,
         out_specs=[vmem, vmem],
         scratch_shapes=[
             pltpu.VMEM((chan_count, rows, depth), jnp.bfloat16),
@@ -252,15 +255,20 @@
             pltpu.VMEM(out_weight.shape, jnp.bfloat16),
             pltpu.VMEM((3, rows, chans), jnp.float32),
             pltpu.VMEM((1, rows, chans), jnp.float32),
-            pltpu.SemaphoreType.DMA((4,)),
+            pltpu.SemaphoreType.DMA((6,)),
             pltpu.SemaphoreType.DMA((2, chan_count)),
             pltpu.SemaphoreType.DMA((2, chan_count)),
             pltpu.SemaphoreType.DMA((3, seq_count)),
             pltpu.SemaphoreType.DMA((3, seq_count)),
             pltpu.SemaphoreType.DMA((3,)),
         ],
+        cost_estimate=pl.CostEstimate(
+            flops=2 * rows * depth * chan_count * chans * 4,
+            bytes_accessed=2 * depth * chan_count * chans * 4,
+            transcendentals=0,
+        ),
         compiler_params=pltpu.CompilerParams(
-            collective_id=0, has_side_effects=True, vmem_limit_bytes=40 * 2**20
+            collective_id=0, has_side_effects=True, vmem_limit_bytes=55 * 2**20
         ),
     )(tokens, cotangent, weights, out_weight, filters)
 
@@ -494,7 +502,7 @@
         + [pltpu.SemaphoreType.DMA((2, outer_count))] * 4
         + [pltpu.SemaphoreType.DMA((2,))],
         compiler_params=pltpu.CompilerParams(
-            collective_id=1, has_side_effects=True, vmem_limit_bytes=44 * 2**20
+            collective_id=1, has_side_effects=True, vmem_limit_bytes=58 * 2**20
         ),
     )(second, grads, weights, out_weight)
 

time: 92.6 us -> 95.6 us (1.032)
  Pallas kernels: 84.5 us -> 87 us
    pallas_call x1, Pallas kernels: 38.7 us -> 40 us  [output_sums(): pl.pallas_call(functools.partial(output_kernel, chan_count, seq_count), o...]
    pallas_call x1, Pallas kernels: 39.7 us -> 40.8 us  [project(): pl.pallas_call(functools.partial(project_kernel, chan_count, seq_count),...]
    unnamed x22 -> x20, local copies, waits for them, and re-layouts: 6.41 us -> 6.82 us
where the time goes in v5:
time: 95.6 us; the launch traced here: 95.4 us
  Pallas kernels  87 us (91%)
  local copies, waits for them, and re-layouts  7.66 us (8%)
    pallas_call x1, Pallas kernels, project(): pl.pallas_call(functools.partial(project_kernel, chan_count, seq_count),...  40.8 us
    pallas_call x1, Pallas kernels, output_sums(): pl.pallas_call(functools.partial(output_kernel, chan_count, seq_count), o...  40 us
    unnamed x20, local copies, waits for them, and re-layouts  6.82 us
    pallas_call x1, Pallas kernels, fused_middle(): pl.pallas_call(middle_kernel, out_shape=[jax.ShapeDtypeStruct((length, la...  6.15 us

profile of v5, /device:TPU:0, one launch (start us, length us, event | category | flops | bytes accessed | tf_op | source)
XLA Modules:
  0.0 95.4 jit_solution(8872654234624141197)
XLA Ops:
  0.6 0.0 copy-start
  0.6 0.0 copy-start.1
  0.7 0.0 copy-start.2
  0.7 0.0 copy-start.3
  0.7 0.0 copy-start.4
  0.7 0.8 constant_dynamic-slice_fusion.skip
  1.5 0.0 copy-done
  1.5 40.8 %shard_map.122 = (f32[4,4,128,128]{3,2,1,0:T(8,128)}, f32[2,4,128,128]{3,2,1,0:T(8,128)}) custom-call(bf16[128,512]{1,0:T(8,128)(2,1)} %tok.1, bf16[128,512]{1,0:T(8,128)(2,1)} %cot.1, bf16[3,4096,512]{2,1,0:T(8,128)(2,1)} %bitcast.9, bf16[512,4096]{1,0:T(8,128)(2,1)} %ow.3, f32[2,128,512]{2,1,0:T(8,128)} %filters.1), custom_call_target="tpu_custom_call" | custom-call | flops 2147483648 | bytes 16777216 | tf_op jit(solution)/shard_map/pallas_call | solution.py:243
  42.3 0.0 copy-done.1
  42.4 0.0 copy-done.2
  42.4 0.0 copy-done.3
  42.4 0.0 copy-done.4
  42.4 0.0 copy-start.5
  42.4 1.2 %copy-done.5 = f32[4,4,128,128]{3,2,1,0:T(8,128)S(1)} copy-done((f32[4,4,128,128]{3,2,1,0:T(8,128)S(1)}, f32[4,4,128,128]{3,2,1,0:T(8,128)}, u32[]{:S(2)}) %copy-start.5) | copy-done | bytes 1048600
  43.6 0.0 copy-start.6
  43.6 1.0 %copy-done.6 = f32[2,4,128,128]{3,2,1,0:T(8,128)S(1)} copy-done((f32[2,4,128,128]{3,2,1,0:T(8,128)S(1)}, f32[2,4,128,128]{3,2,1,0:T(8,128)}, u32[]{:S(2)}) %copy-start.6) | copy-done | bytes 524312
  44.7 6.2 %shard_map.123 = (bf16[512,128]{1,0:T(8,128)(2,1)S(1)}, bf16[3,512,128]{2,1,0:T(8,128)(2,1)S(1)}) custom-call(f32[4,512,128]{2,1,0:T(8,128)S(1)} %bitcast.5, f32[2,512,128]{2,1,0:T(8,128)S(1)} %bitcast.6, f32[3,3,128]{2,1,0:T(4,128)S(1)} %constant_dynamic-slice_fusion.1.taps, f32[2,128]{1,0:T(2,128)S(1)} %constant_dynamic-slice_fusion.skip, ...), custom_call_target="tpu_custom_call" | custom-call | tf_op jit(solution)/shard_map/pallas_call | solution.py:338
  50.8 0.0 copy-start.7
  50.8 0.7 copy-done.7
  51.6 0.0 copy-start.8
  51.6 0.7 copy-done.8
  52.2 40.0 %shard_map.124 = (bf16[128,512]{1,0:T(8,128)(2,1)}, bf16[128,512]{1,0:T(8,128)(2,1)}) custom-call(bf16[4,128,128]{2,1,0:T(8,128)(2,1)} %bitcast.8, bf16[3,4,128,128]{3,2,1,0:T(8,128)(2,1)} %bitcast.7, bf16[3,4096,512]{2,1,0:T(8,128)(2,1)} %bitcast.10, bf16[512,4096]{1,0:T(8,128)(2,1)} %ow.3), custom_call_target="tpu_custom_call" | custom-call | tf_op jit(solution)/shard_map/pallas_call | solution.py:484
  92.3 1.6 %copy.15 = bf16[128,512]{1,0:T(8,128)(2,1)} copy(bf16[128,512]{1,0:T(8,128)(2,1)} %get-tuple-element.12) | data formatting | bytes 262144
  93.8 1.6 %copy.16 = bf16[128,512]{1,0:T(8,128)(2,1)} copy(bf16[128,512]{1,0:T(8,128)(2,1)} %get-tuple-element.13) | data formatting | bytes 262144
  (1 shorter events, 0.0 us)
Async XLA Ops:
  0.6 0.9 copy-start
  0.6 41.7 %copy-start.1 = (bf16[512,1024]{1,0:T(8,128)(2,1)S(1)}, bf16[512,1024]{1,0:T(8,128)(2,1)}, u32[]{:S(2)}) copy-start(bf16[512,1024]{1,0:T(8,128)(2,1)} %constant.22.clone.back_low) | copy-start | bytes 3145732
  0.7 41.7 %copy-start.2 = (bf16[512,1024]{1,0:T(8,128)(2,1)S(1)}, bf16[512,1024]{1,0:T(8,128)(2,1)}, u32[]{:S(2)}) copy-start(bf16[512,1024]{1,0:T(8,128)(2,1)} %constant.21.clone.back_high) | copy-start | bytes 3145732
  0.7 41.7 %copy-start.3 = (bf16[1024,512]{1,0:T(8,128)(2,1)S(1)}, bf16[1024,512]{1,0:T(8,128)(2,1)}, u32[]{:S(2)}) copy-start(bf16[1024,512]{1,0:T(8,128)(2,1)} %constant.20.clone.low) | copy-start | bytes 3145732
  0.7 41.7 %copy-start.4 = (bf16[1024,512]{1,0:T(8,128)(2,1)S(1)}, bf16[1024,512]{1,0:T(8,128)(2,1)}, u32[]{:S(2)}) copy-start(bf16[1024,512]{1,0:T(8,128)(2,1)} %constant.19.clone.high) | copy-start | bytes 3145732
  42.4 1.2 %copy-start.5 = (f32[4,4,128,128]{3,2,1,0:T(8,128)S(1)}, f32[4,4,128,128]{3,2,1,0:T(8,128)}, u32[]{:S(2)}) copy-start(f32[4,4,128,128]{3,2,1,0:T(8,128)} %get-tuple-element.6) | copy-start | bytes 3145732
  43.6 1.0 %copy-start.6 = (f32[2,4,128,128]{3,2,1,0:T(8,128)S(1)}, f32[2,4,128,128]{3,2,1,0:T(8,128)}, u32[]{:S(2)}) copy-start(f32[2,4,128,128]{3,2,1,0:T(8,128)} %get-tuple-element.7) | copy-start | bytes 1572868
  50.8 0.7 copy-start.7
  51.6 0.7 copy-start.8
